TPU v7x, 32 devices: a whole 2x2x4 slice. The times are simulated.
32 devices in a mesh: row: 4 (over x, core), col: 8 (over z, y).
Axes of the slice: x: 2, y: 2, z: 4, core: 2. Of those that a mesh axis runs over, the one named last changes fastest.
Arguments:
- strain_rate: bfloat16 [512, 64, 1024], P(('row', 'col')), may hold values from -200 to 200
Outputs:
- cross_spectra: bfloat16 [2, 4, 8, 4, 16, 512], P(None, None, 'col', None, None, 'row')
All inputs are finite; a program needn't handle non-finite values.
Results may differ from a plain program's by a relative error of at most 0.0064.
Values may be sent and summed in bfloat16 or wider, within the bound.
No kernel may reach another device: no remote copies, remote signals or barrier semaphores. Data moves between devices by JAX's collectives and lax.ppermute only.
A program may use at most 64 MiB of HBM per device.

v0:
```python
import math

import jax
import jax.numpy as jnp
from jax import lax
from jax.sharding import PartitionSpec as P

W = 64
NS = 1024
HALF = 64
K0 = 6
FS = 4
SMOOTH = 4


def dft_table():
    sample_index = jnp.arange(NS, dtype=jnp.int32)
    bin_index = K0 + jnp.arange(FS + 2 * SMOOTH, dtype=jnp.int32)
    phases = (sample_index[:, None] * bin_index[None, :] % NS).astype(jnp.float32) * (
        2.0 * math.pi / NS
    )
    return jnp.concatenate([jnp.cos(phases), -jnp.sin(phases)], axis=1) / math.sqrt(NS)


def whiten(spectrum):
    bands = FS + 2 * SMOOTH
    real_part = spectrum[..., :bands]
    imag_part = spectrum[..., bands:]
    magnitude = jnp.sqrt(real_part * real_part + imag_part * imag_part)
    smoothed = magnitude[..., 0:FS]
    for offset in range(1, 2 * SMOOTH + 1):
        smoothed = smoothed + magnitude[..., offset : offset + FS]
    divisor = jnp.maximum(smoothed / (2 * SMOOTH + 1), 0.6)
    white_real = real_part[..., SMOOTH : SMOOTH + FS] / divisor
    white_imag = imag_part[..., SMOOTH : SMOOTH + FS] / divisor
    return jnp.stack([white_real, white_imag]).astype(jnp.bfloat16).transpose(0, 3, 2, 1)


def prepare(window_block):
    channels, windows, samples = window_block.shape
    sample_index = jnp.arange(NS, dtype=jnp.int32)
    band_matrix = (jnp.abs(sample_index[:, None] - sample_index[None, :]) <= HALF).astype(
        jnp.bfloat16
    )
    counts = (
        jnp.minimum(sample_index + HALF, NS - 1) - jnp.maximum(sample_index - HALF, 0) + 1
    ).astype(jnp.float32)
    running = jnp.dot(
        jnp.abs(window_block).reshape(-1, NS), band_matrix, preferred_element_type=jnp.float32
    )
    flattened = window_block.reshape(-1, NS).astype(jnp.float32) / (running / counts + 1e-06)
    spectrum = jnp.dot(flattened, dft_table(), precision=lax.Precision.HIGHEST)
    return whiten(spectrum.reshape(channels, windows, -1))


def apply_weight(spectra, gain_square):
    return (spectra.astype(jnp.float32) * gain_square[None, None, :, None]).astype(jnp.bfloat16)


def cross_terms(column_side, shard_piece):
    real_sum = jnp.einsum(
        "fwb,fwa->fba", column_side[0], shard_piece[0], preferred_element_type=jnp.float32
    )
    real_sum = real_sum + jnp.einsum(
        "fwb,fwa->fba", column_side[1], shard_piece[1], preferred_element_type=jnp.float32
    )
    imag_sum = jnp.einsum(
        "fwb,fwa->fba", column_side[0], shard_piece[1], preferred_element_type=jnp.float32
    )
    imag_sum = imag_sum - jnp.einsum(
        "fwb,fwa->fba", column_side[1], shard_piece[0], preferred_element_type=jnp.float32
    )
    return jnp.stack([real_sum, imag_sum])


def shards(strain_rate):
    channels, windows, samples = strain_rate.shape
    row_count = lax.axis_size("row")
    col_count = lax.axis_size("col")
    local_power = jnp.sum(jnp.square(strain_rate.astype(jnp.float32)), axis=(0, 2))
    window_power = lax.psum(local_power, ("row", "col")) / (
        channels * row_count * col_count * samples
    )
    window_gain = 1.0 / jnp.sqrt(window_power + 1e-05)
    gain_square = window_gain * window_gain
    own_spectra = prepare(strain_rate)
    outgoing = apply_weight(own_spectra, gain_square)
    gathered = lax.all_gather(outgoing, "row", axis=3, tiled=True)
    tile_sum = cross_terms(gathered, lax.all_gather(own_spectra, "col", axis=3, tiled=True))
    result = (tile_sum / W).astype(jnp.bfloat16)
    return result.reshape(2, FS, 1, row_count, channels, -1)


def solution(mesh):
    return jax.shard_map(
        shards,
        mesh=mesh,
        in_specs=(P(("row", "col"), None, None),),
        out_specs=P(None, None, "col", None, None, "row"),
        check_vma=False,
    )
```

profile of v0, /device:TPU:0, one launch (start us, length us, event | category | flops | bytes accessed | tf_op | source)
XLA Modules:
  0.0 89.6 jit_solution(5842348181047815657)
XLA Ops:
  0.0 0.0 copy-start
  0.0 2.4 %abs.7 = bf16[16,64,1024]{2,1,0:T(8,128)(2,1)S(1)} abs(bf16[16,64,1024]{2,1,0:T(8,128)(2,1)} %param.1) | non-fusion elementwise | flops 1048576 | bytes 4194304 | tf_op jit(solution)/shard_map/abs | solution.py:49
  2.4 0.0 copy-done
  2.4 2.7 %bitcast_divide_fusion = f32[1024,1024]{1,0:T(8,128)S(1)} fusion(f32[1024]{0:T(1024)S(1)} %fusion.31, bf16[1024,1024]{1,0:T(8,128)(2,1)S(1)} %bitcast.42, bf16[16,64,1024]{2,1,0:T(8,128)(2,1)S(1)} %copy-done), kind=kOutput, calls=%fused_computation | convolution fusion | flops 2154823680 | bytes 8392704 | tf_op jit(solution)/shard_map/dot_general | solution.py:48
  5.1 0.3 fusion.25
  5.5 3.6 %fusion.5 = f32[1024,24]{0,1:T(8,128)S(1)} fusion(f32[1024,1024]{1,0:T(8,128)S(1)} %bitcast_divide_fusion, f32[1024,12]{0,1:T(8,128)S(1)} %get-tuple-element.12, f32[1024,12]{0,1:T(8,128)S(1)} %get-tuple-element.11), kind=kOutput, calls=%fused_computation.14 | convolution fusion | flops 302039040 | bytes 4390912 | tf_op jit(solution)/shard_map/dot_general | solution.py:52
  9.1 0.1 reshape.61
  9.4 32.5 %all_gather.7 = bf16[2,4,64,128]{2,1,0,3:T(4,128)(2,1)S(1)} all-gather(bf16[2,4,64,16]{2,1,0,3:T(4,128)(2,1)S(1)} %bitcast.45), channel_id=1, replica_groups=mesh['row'=4,'col'=8] {'col'}, dimensions={3}, use_global_device_ids=true | all-gather | bytes 147456 | tf_op jit(solution)/shard_map/all_gather | solution.py:89
  41.9 0.1 fusion.37
  42.0 0.1 copy.22
  42.1 0.5 multiply_reduce_fusion
  42.6 39.7 %psum.7 = f32[64]{0:T(128)S(1)} all-reduce(f32[64]{0:T(128)S(1)} %multiply_reduce_fusion), channel_id=1, replica_groups=mesh['row'=4,'col'=8] {'row','col'}, use_global_device_ids=true, to_apply=%region_1.0 | all-reduce | flops 64 | bytes 512 | tf_op jit(solution)/shard_map/psum | solution.py:81
  82.3 5.8 %all_gather.6 = bf16[2,4,64,64]{2,1,0,3:T(4,128)(2,1)S(1)} all-gather(bf16[2,4,64,16]{2,1,0,3:T(4,128)(2,1)S(1)} %multiply_convert_fusion), channel_id=1, replica_groups=mesh['row'=4,'col'=8] {'row'}, dimensions={3}, use_global_device_ids=true | all-gather | bytes 81920 | tf_op jit(solution)/shard_map/all_gather | solution.py:88
  88.2 0.1 fusion.11
  88.4 0.1 copy.20
  88.5 0.2 convolution_subtract_fusion
  88.6 0.1 fusion.15
  88.8 0.2 convolution_add_fusion
  88.9 0.7 fusion.2
  (10 shorter events, 0.2 us)
Async XLA Ops:
  0.0 2.4 %copy-start = (bf16[16,64,1024]{2,1,0:T(8,128)(2,1)S(1)}, bf16[16,64,1024]{2,1,0:T(8,128)(2,1)}, u32[]{:S(2)}) copy-start(bf16[16,64,1024]{2,1,0:T(8,128)(2,1)} %param.1) | copy-start | bytes 6291460
where the time goes:
time: 90 us; the launch traced here: 89.6 us
  blocking collectives  78 us (87%)
  matrix products  6.93 us (8%)
  other arithmetic  4.07 us (5%)
    psum x1, blocking collectives, shards(): lax.psum(local_power, ('row', 'col'))  39.7 us
    all_gather x1, blocking collectives, shards(): lax.all_gather(own_spectra, 'col', axis=3, tiled=True)  32.5 us
    all_gather x1, blocking collectives, shards(): gathered = lax.all_gather(outgoing, 'row', axis=3, tiled=True)  5.82 us
    dot_general x1, matrix products, prepare(): spectrum = jnp.dot(flattened, dft_table(), precision=lax.Precision.HIGHEST)  3.63 us
    dot_general x1, matrix products, prepare(): jnp.dot(jnp.abs(window_block).reshape(-1, NS), band_matrix, preferred_ele...  2.71 us
    abs x1, other arithmetic, prepare(): jnp.abs(window_block).reshape(-1, NS)  2.39 us

commit v1 on v0

v1 whole, which is shorter than its diff:
```python
import functools
import math

import jax
import jax.numpy as jnp
import numpy as np
from jax import lax
from jax.experimental import pallas as pl
from jax.experimental.pallas import tpu as pltpu
from jax.sharding import PartitionSpec as P

W = 64
NS = 1024
HALF = 64
K0 = 6
FS = 4
SMOOTH = 4
BANDS = FS + 2 * SMOOTH
PAD = 16
TILE = 256
REACH = 128
LANES = 2 * W
POWER_ROWS = 16

BF16 = jnp.bfloat16
F32 = jnp.float32


def sample_counts():
    sample = np.arange(NS)
    return np.minimum(sample + HALF, NS - 1) - np.maximum(sample - HALF, 0) + 1


def band_block():
    source = np.arange(-REACH, TILE + REACH)[:, None]
    return jnp.asarray(np.abs(source - np.arange(TILE)[None, :]) <= HALF, BF16)


def dft_rows():
    phase = np.outer(K0 + np.arange(BANDS), np.arange(NS)) % NS * (2.0 * math.pi / NS)
    scale = sample_counts() / math.sqrt(NS)
    table = np.zeros((2 * PAD, NS), np.float64)
    table[:BANDS] = np.cos(phase) * scale
    table[PAD : PAD + BANDS] = -np.sin(phase) * scale
    high = table.astype(BF16)
    low = (table - high.astype(np.float64)).astype(BF16)
    return jnp.asarray(np.concatenate([high, low], axis=0))


def count_row():
    return jnp.asarray(sample_counts()[None, :] * 1e-06, F32)


def power_kernel(x_ref, out_ref, total):
    step = pl.program_id(0)

    @pl.when(step == 0)
    def _():
        total[...] = jnp.zeros_like(total)

    partial = None
    for channel in range(x_ref.shape[0]):
        for tile in range(NS // 128):
            value = x_ref[channel, :, tile * 128 : (tile + 1) * 128].astype(F32)
            square = value * value
            partial = square if partial is None else partial + square
    total[...] += partial

    @pl.when(step == pl.num_programs(0) - 1)
    def _():
        columns = jnp.transpose(total[...])
        row = jnp.sum(columns, axis=0, keepdims=True)
        out_ref[...] = jnp.broadcast_to(jnp.concatenate([row, row], axis=1), out_ref.shape)


def local_power(strain_rate, block=4):
    channels = strain_rate.shape[0]
    return pl.pallas_call(
        power_kernel,
        grid=(channels // block,),
        in_specs=[pl.BlockSpec((block, W, NS), lambda i: (i, 0, 0))],
        out_specs=pl.BlockSpec((8, LANES), lambda i: (0, 0)),
        out_shape=jax.ShapeDtypeStruct((8, LANES), F32),
        scratch_shapes=[pltpu.VMEM((W, 128), F32)],
        compiler_params=pltpu.CompilerParams(vmem_limit_bytes=8 * 2**20),
        name="power",
    )(strain_rate)


def whiten_rows(spectrum):
    real_part = spectrum[:BANDS]
    imag_part = spectrum[PAD : PAD + BANDS]
    magnitude = jnp.sqrt(real_part * real_part + imag_part * imag_part)
    smoothed = magnitude[0:FS]
    for offset in range(1, 2 * SMOOTH + 1):
        smoothed = smoothed + magnitude[offset : offset + FS]
    divisor = jnp.maximum(smoothed * (1.0 / (2 * SMOOTH + 1)), 0.6)
    return real_part[SMOOTH : SMOOTH + FS] / divisor, imag_part[SMOOTH : SMOOTH + FS] / divisor


def spectra_kernel(x_ref, band_ref, dft_ref, count_ref, out_ref, rows):
    step = pl.program_id(0)
    block = x_ref.shape[0]
    x = x_ref[...].reshape(block * W, NS)
    magnitude = jnp.abs(x)
    spectrum = None
    for tile in range(NS // TILE):
        start, stop = tile * TILE, (tile + 1) * TILE
        low, high = max(start - REACH, 0), min(stop + REACH, NS)
        skip = low - (start - REACH)
        running = jnp.dot(
            magnitude[:, low:high],
            band_ref[skip : skip + high - low, :],
            preferred_element_type=F32,
        )
        flat = x[:, start:stop].astype(F32) / (running + count_ref[:, start:stop])
        flat_high = flat.astype(BF16)
        flat_low = (flat - flat_high.astype(F32)).astype(BF16)
        dims = (((1,), (1,)), ((), ()))
        both = lax.dot_general(
            dft_ref[:, start:stop], flat_high, dims, preferred_element_type=F32
        )
        rest = lax.dot_general(
            dft_ref[: 2 * PAD, start:stop], flat_low, dims, preferred_element_type=F32
        )
        term = both[: 2 * PAD] + (both[2 * PAD :] + rest)
        spectrum = term if spectrum is None else spectrum + term
    white_real, white_imag = whiten_rows(spectrum)
    first_half = lax.broadcasted_iota(jnp.int32, (FS, LANES), 1) < W
    for pair in range(block // 2):
        real = white_real[:, pair * LANES : (pair + 1) * LANES]
        imag = white_imag[:, pair * LANES : (pair + 1) * LANES]
        even = jnp.where(first_half, real, pltpu.roll(imag, W, 1))
        odd = jnp.where(first_half, pltpu.roll(real, W, 1), imag)
        for bin_number in range(FS):
            channel = step * block + 2 * pair
            rows[bin_number, pl.ds(channel, 1), :] = even[bin_number : bin_number + 1]
            rows[bin_number, pl.ds(channel + 1, 1), :] = odd[bin_number : bin_number + 1]

    @pl.when(step == pl.num_programs(0) - 1)
    def _():
        out_ref[...] = rows[...].astype(BF16)


def local_spectra(strain_rate, block=4):
    channels = strain_rate.shape[0]
    whole = lambda i: (0, 0)
    return pl.pallas_call(
        spectra_kernel,
        grid=(channels // block,),
        in_specs=[
            pl.BlockSpec((block, W, NS), lambda i: (i, 0, 0)),
            pl.BlockSpec((TILE + 2 * REACH, TILE), whole),
            pl.BlockSpec((4 * PAD, NS), whole),
            pl.BlockSpec((1, NS), whole),
        ],
        out_specs=pl.BlockSpec((FS, channels, LANES), lambda i: (0, 0, 0)),
        out_shape=jax.ShapeDtypeStruct((FS, channels, LANES), BF16),
        scratch_shapes=[pltpu.VMEM((FS, channels, LANES), F32)],
        compiler_params=pltpu.CompilerParams(vmem_limit_bytes=40 * 2**20),
        name="spectra",
    )(strain_rate, band_block(), dft_rows(), count_row())


def cross_kernel(order, members, samples, me_ref, gathered_ref, own_ref, *refs):
    *row_refs, out_ref, first, second = refs
    channels = own_ref.shape[1]
    rows = FS * channels
    power = None
    for block in range(len(order)):
        parts = gathered_ref[block, rows : rows + POWER_ROWS, :].astype(F32)
        value = parts[0:1] + (parts[1:2] + parts[2:3])
        power = value if power is None else power + value
    power = power / (channels * members * samples)
    gain = 1.0 / jnp.sqrt(power + 1e-05)
    gain_square = gain * gain
    lane = lax.broadcasted_iota(jnp.int32, (1, LANES), 1)
    turned_gain = jnp.where(lane < W, -gain_square, gain_square)
    me = me_ref[0]
    for shift, ref in enumerate((own_ref, *row_refs)):
        row = jnp.bitwise_xor(me, shift)
        place = pl.ds(pl.multiple_of(row * channels, channels), channels)
        for bin_number in range(FS):
            value = ref[bin_number].astype(F32)
            second[0, bin_number, place, :] = (value * gain_square).astype(BF16)
            second[1, bin_number, place, :] = (pltpu.roll(value, W, 1) * turned_gain).astype(BF16)
    for block, column in enumerate(order):
        for bin_number in range(FS):
            first[bin_number, column * channels : (column + 1) * channels, :] = gathered_ref[
                block, bin_number * channels : (bin_number + 1) * channels, :
            ]
    for bin_number in range(FS):
        for part in range(2):
            total = lax.dot_general(
                second[part, bin_number],
                first[bin_number],
                (((1,), (1,)), ((), ())),
                preferred_element_type=F32,
            )
            out_ref[part, bin_number] = (total * (1.0 / W)).astype(BF16)


def column_order(col_count):
    best = [4, 0, 5, 6, 1, 2, 7, 3]
    if col_count == len(best):
        return best
    middle = col_count // 2
    return [middle, *(c for c in range(col_count) if c != middle)]


def split_three(value):
    high = lax.reduce_precision(value, 8, 7)
    rest = value - high
    middle = lax.reduce_precision(rest, 8, 7)
    return high.astype(BF16), middle.astype(BF16), (rest - middle).astype(BF16)


def shards(strain_rate):
    channels, windows, samples = strain_rate.shape
    row_count = lax.axis_size("row")
    col_count = lax.axis_size("col")
    order = column_order(col_count)

    def from_row(value, shift):
        return lax.ppermute(value, "row", [(i, i ^ shift) for i in range(row_count)])

    own_power = local_power(strain_rate)
    row_power = own_power
    for shift in range(1, row_count):
        row_power = row_power + from_row(own_power, shift)
    spectra = local_spectra(strain_rate)
    power_rows = jnp.concatenate(
        [part[:1] for part in split_three(row_power)]
        + [jnp.zeros((POWER_ROWS - 3, LANES), BF16)],
        axis=0,
    )
    message = jnp.concatenate([spectra.reshape(FS * channels, LANES), power_rows], axis=0)
    gathered = lax.all_to_all(
        jnp.broadcast_to(message, (col_count, *message.shape)), "col", 0, 0, axis_index_groups=[order]
    )
    others = [from_row(spectra, shift) for shift in range(1, row_count)]
    me = lax.axis_index("row").astype(jnp.int32).reshape(1)
    result = pl.pallas_call(
        functools.partial(cross_kernel, order, row_count * col_count, samples),
        in_specs=[pl.BlockSpec(memory_space=pltpu.SMEM)]
        + [pl.BlockSpec(memory_space=pltpu.VMEM)] * (2 + len(others)),
        out_specs=pl.BlockSpec(memory_space=pltpu.VMEM),
        out_shape=jax.ShapeDtypeStruct(
            (2, FS, row_count * channels, col_count * channels), BF16
        ),
        scratch_shapes=[
            pltpu.VMEM((FS, col_count * channels, LANES), BF16),
            pltpu.VMEM((2, FS, row_count * channels, LANES), BF16),
        ],
        compiler_params=pltpu.CompilerParams(vmem_limit_bytes=8 * 2**20),
        name="cross",
    )(me, gathered, spectra, *others)
    return result.reshape(2, FS, 1, row_count, channels, -1)


def solution(mesh):
    return jax.shard_map(
        shards,
        mesh=mesh,
        in_specs=(P(("row", "col"), None, None),),
        out_specs=P(None, None, "col", None, None, "row"),
        check_vma=False,
    )
```

time: 90 us -> 24.6 us (0.27)
  blocking collectives: 78 us -> 0 us
  starting transfers between devices: 0 us -> 11.6 us
  matrix products: 6.93 us -> 0 us
  Pallas kernels: 0 us -> 5.23 us
  other arithmetic: 4.07 us -> 0.02 us
  local copies, waits for them, and re-layouts: 0.49 us -> 4.31 us
  waiting for transfers between devices: 0 us -> 3.11 us
    psum x1 -> x0, blocking collectives: 39.7 us -> none  [shards(): lax.psum(local_power, ('row', 'col'))]
    all_gather x2 -> x0, blocking collectives: 38.3 us -> none  [the longest x1 32.5 us: shards(): lax.all_gather(own_spectra, 'col', axis=3, tiled=True)]
    dot_general x6 -> x0, matrix products: 6.93 us -> none  [the longest x1 3.63 us: prepare(): spectrum = jnp.dot(flattened, dft_table(), precision=lax.Precision.HIGHEST)]
    all_to_all x0 -> x1, starting transfers between devices: none -> 6.63 us  [shards(): lax.all_to_all(jnp.broadcast_to(message, (col_count, *message.shape)), 'c...]
    pallas_call x0 -> x3, Pallas kernels: none -> 5.23 us  [the longest x1 3.57 us: local_spectra(): pl.pallas_call(spectra_kernel, grid=(channels // block,), in_specs=[pl.Bl...]
    ppermute x0 -> x6, starting transfers between devices: none -> 4.96 us  [from_row(): lax.ppermute(value, 'row', [(i, i ^ shift) for i in range(row_count)])]
    unnamed x4 -> x10, local copies, waits for them, and re-layouts: 0.24 us -> 3.45 us
    ppermute x0 -> x6, waiting for transfers between devices: none -> 2.8 us  [from_row(): lax.ppermute(value, 'row', [(i, i ^ shift) for i in range(row_count)])]
  transfers between devices with their start and end apart: 0 -> 7, of which waited for: 0 -> 3; matrix products, arithmetic and copies ran while one was open for 0% -> 0% of each run, Pallas kernels for 0% -> 15%
where the time goes in v1:
time: 24.6 us; the launch traced here: 24.3 us
  starting transfers between devices  11.6 us (47%)
  Pallas kernels  5.23 us (21%)
  local copies, waits for them, and re-layouts  4.31 us (18%)
  waiting for transfers between devices  3.11 us (13%)
    all_to_all x1, starting transfers between devices, shards(): lax.all_to_all(jnp.broadcast_to(message, (col_count, *message.shape)), 'c...  6.63 us
    ppermute x6, starting transfers between devices, from_row(): lax.ppermute(value, 'row', [(i, i ^ shift) for i in range(row_count)])  4.96 us
    pallas_call x1, Pallas kernels, local_spectra(): pl.pallas_call(spectra_kernel, grid=(channels // block,), in_specs=[pl.Bl...  3.57 us
    unnamed x10, local copies, waits for them, and re-layouts  3.45 us
    ppermute x6, waiting for transfers between devices, from_row(): lax.ppermute(value, 'row', [(i, i ^ shift) for i in range(row_count)])  2.8 us
    pallas_call x1, Pallas kernels, shards(): pl.pallas_call(functools.partial(cross_kernel, order, row_count * col_cou...  1.01 us
    broadcast_in_dim x1, local copies, waits for them, and re-layouts, shards(): jnp.broadcast_to(message, (col_count, *message.shape))  0.69 us
    pallas_call x1, Pallas kernels, local_power(): pl.pallas_call(power_kernel, grid=(channels // block,), in_specs=[pl.Bloc...  0.66 us
  transfers between devices with their start and end apart: 7, of which 3 were waited for; matrix products, arithmetic and copies ran while one was open for 0% of the time, Pallas kernels for 15%

profile of v1, /device:TPU:0, one launch (start us, length us, event | category | flops | bytes accessed | tf_op | source)
XLA Modules:
  0.0 24.3 jit_solution(18007671073738933989)
XLA Ops:
  0.0 0.0 copy-start
  0.0 1.6 %copy-done = bf16[16,64,1024]{2,1,0:T(8,128)(2,1)S(1)} copy-done((bf16[16,64,1024]{2,1,0:T(8,128)(2,1)S(1)}, bf16[16,64,1024]{2,1,0:T(8,128)(2,1)}, u32[]{:S(2)}) %copy-start) | copy-done | bytes 2097176
  1.6 0.0 copy-start.1
  1.6 0.0 copy-start.4
  1.6 0.7 %power.1 = f32[8,128]{1,0:T(8,128)S(1)} custom-call(bf16[16,64,1024]{2,1,0:T(8,128)(2,1)S(1)} %copy-done), custom_call_target="tpu_custom_call" | custom-call | tf_op jit(solution)/shard_map/power/pallas_call | solution.py:78
  2.3 0.5 %collective-permute-start = (f32[8,128]{1,0:T(8,128)S(1)}, f32[8,128]{1,0:T(8,128)S(1)}, u32[]{:S(2)}, u32[]{:S(2)}) collective-permute-start(f32[8,128]{1,0:T(8,128)S(1)} %power.1), channel_id=1, source_target_pairs={{0,8},{8,0},{16,24},{24,16},{1,9},{9,1},{17,25},{25,17},{2,10},{10... | collective-permute-start | bytes 12296 | tf_op jit(solution)/shard_map/ppermute | solution.py:225
  2.7 2.6 %collective-permute-start.1 = (f32[8,128]{1,0:T(8,128)S(1)}, f32[8,128]{1,0:T(8,128)S(1)}, u32[]{:S(2)}, u32[]{:S(2)}) collective-permute-start(f32[8,128]{1,0:T(8,128)S(1)} %power.1), channel_id=1, source_target_pairs={{0,16},{8,24},{16,0},{24,8},{1,17},{9,25},{17,1},{25,9},{2,18},{10... | collective-permute-start | bytes 12296 | tf_op jit(solution)/shard_map/ppermute | solution.py:225
  5.3 0.1 collective-permute-start.2
  5.4 0.0 copy-done.1
  5.4 0.0 copy-done.4
  5.4 0.0 copy-start.2
  5.4 0.9 %copy-done.2 = bf16[512,256]{1,0:T(8,128)(2,1)S(1)} copy-done((bf16[512,256]{1,0:T(8,128)(2,1)S(1)}, bf16[512,256]{1,0:T(8,128)(2,1)}, u32[]{:S(2)}) %copy-start.2) | copy-done | bytes 262168
  6.3 0.0 copy-start.3
  6.3 0.9 %copy-done.3 = bf16[64,1024]{1,0:T(8,128)(2,1)S(1)} copy-done((bf16[64,1024]{1,0:T(8,128)(2,1)S(1)}, bf16[64,1024]{1,0:T(8,128)(2,1)}, u32[]{:S(2)}) %copy-start.3) | copy-done | bytes 131096
  7.2 3.6 %spectra.1.own_ref = bf16[4,16,128]{2,1,0:T(8,128)(2,1)S(1)} custom-call(bf16[16,64,1024]{2,1,0:T(8,128)(2,1)S(1)} %copy-done.1, bf16[512,256]{1,0:T(8,128)(2,1)S(1)} %copy-done.2, bf16[64,1024]{1,0:T(8,128)(2,1)S(1)} %copy-done.3, f32[1,1024]{1,0:T(1,128)S(1)} %copy-done.4), custom_call_target="tpu_custom_call" | custom-call | tf_op jit(solution)/shard_map/spectra/pallas_call | solution.py:148
  10.8 0.0 collective-permute-done
  10.8 0.0 collective-permute-done.1
  10.8 0.0 collective-permute-done.2
  10.9 0.2 concatenate.3
  11.1 0.7 %broadcast_in_dim.7 = bf16[8,80,128]{2,1,0:T(8,128)(2,1)} broadcast(bf16[80,128]{1,0:T(8,128)(2,1)S(1)} %concatenate.3), dimensions={1,2} | broadcast | bytes 184320 | tf_op jit(solution)/shard_map/broadcast_in_dim | solution.py:239
  11.7 6.6 %all-to-all-start = ((bf16[8,80,128]{2,1,0:T(8,128)(2,1)}), bf16[8,80,128]{2,1,0:T(8,128)(2,1)S(1)}, u32[]{:S(2)}, u32[]{:S(2)}) async-start(bf16[8,80,128]{2,1,0:T(8,128)(2,1)} %broadcast_in_dim.7), calls=%async_computation | async-start | bytes 327680 | tf_op jit(solution)/shard_map/all_to_all | solution.py:238
  18.4 0.0 collective-permute-start.3
  18.4 1.5 %collective-permute-start.4 = (bf16[4,16,128]{2,1,0:T(8,128)(2,1)S(1)}, bf16[4,16,128]{2,1,0:T(8,128)(2,1)S(1)}, u32[]{:S(2)}, u32[]{:S(2)}) collective-permute-start(bf16[4,16,128]{2,1,0:T(8,128)(2,1)S(1)} %spectra.1.own_ref), channel_id=1, source_target_pairs={{0,16},{8,24},{16,0},{24,8},{1,17},{9,25},{17,1},{25,9},{2,18},{10... | collective-permute-start | bytes 49160 | tf_op jit(solution)/shard_map/ppermute | solution.py:225
  19.9 0.4 %collective-permute-start.5 = (bf16[4,16,128]{2,1,0:T(8,128)(2,1)S(1)}, bf16[4,16,128]{2,1,0:T(8,128)(2,1)S(1)}, u32[]{:S(2)}, u32[]{:S(2)}) collective-permute-start(bf16[4,16,128]{2,1,0:T(8,128)(2,1)S(1)} %spectra.1.own_ref), channel_id=1, source_target_pairs={{0,24},{8,16},{16,8},{24,0},{1,25},{9,17},{17,9},{25,1},{2,26},{10... | collective-permute-start | bytes 49160 | tf_op jit(solution)/shard_map/ppermute | solution.py:225
  20.2 0.0 collective-permute-done.3.refs_0_
  20.2 1.9 %collective-permute-done.4.refs_1_ = bf16[4,16,128]{2,1,0:T(8,128)(2,1)S(1)} collective-permute-done((bf16[4,16,128]{2,1,0:T(8,128)(2,1)S(1)}, bf16[4,16,128]{2,1,0:T(8,128)(2,1)S(1)}, u32[]{:S(2)}, u32[]{:S(2)}) %collective-permute-start.4) | collective-permute-done | bytes 16416 | tf_op jit(solution)/shard_map/ppermute | solution.py:225
  22.1 0.9 %collective-permute-done.5.refs_2_ = bf16[4,16,128]{2,1,0:T(8,128)(2,1)S(1)} collective-permute-done((bf16[4,16,128]{2,1,0:T(8,128)(2,1)S(1)}, bf16[4,16,128]{2,1,0:T(8,128)(2,1)S(1)}, u32[]{:S(2)}, u32[]{:S(2)}) %collective-permute-start.5) | collective-permute-done | bytes 16416 | tf_op jit(solution)/shard_map/ppermute | solution.py:225
  23.0 0.3 %all-to-all-done.gathered_ref = bf16[8,80,128]{2,1,0:T(8,128)(2,1)S(1)} async-done(((bf16[8,80,128]{2,1,0:T(8,128)(2,1)}), bf16[8,80,128]{2,1,0:T(8,128)(2,1)S(1)}, u32[]{:S(2)}, u32[]{:S(2)}) %all-to-all-start) | async-done | bytes 163872 | tf_op jit(solution)/shard_map/all_to_all | solution.py:238
  23.3 1.0 %cross.1 = bf16[2,4,64,128]{3,2,1,0:T(8,128)(2,1)} custom-call(s32[1]{0:T(128)} %bitcast.me_ref, bf16[8,80,128]{2,1,0:T(8,128)(2,1)S(1)} %all-to-all-done.gathered_ref, bf16[4,16,128]{2,1,0:T(8,128)(2,1)S(1)} %spectra.1.own_ref, bf16[4,16,128]{2,1,0:T(8,128)(2,1)S(1)} %collective-permute-done.3.refs_0_, ...), custom_call_target="tpu_custom_call" | custom-call | tf_op jit(solution)/shard_map/cross/pallas_call | solution.py:243
  (6 shorter events, 0.0 us)
Async XLA Ops:
  0.0 1.6 %copy-start = (bf16[16,64,1024]{2,1,0:T(8,128)(2,1)S(1)}, bf16[16,64,1024]{2,1,0:T(8,128)(2,1)}, u32[]{:S(2)}) copy-start(bf16[16,64,1024]{2,1,0:T(8,128)(2,1)} %x_ref.3) | copy-start | bytes 6291460
  1.6 3.8 %copy-start.1 = (bf16[16,64,1024]{2,1,0:T(8,128)(2,1)S(1)}, bf16[16,64,1024]{2,1,0:T(8,128)(2,1)}, u32[]{:S(2)}) copy-start(bf16[16,64,1024]{2,1,0:T(8,128)(2,1)} %x_ref.3) | copy-start | bytes 6291460
  1.6 3.8 %copy-start.4 = (f32[1,1024]{1,0:T(1,128)S(1)}, f32[1,1024]{1,0:T(1,128)}, u32[]{:S(2)}) copy-start(f32[1,1024]{1,0:T(1,128)} %constant.15.clone.count_ref) | copy-start | bytes 12292
  2.3 8.5 %collective-permute-start = (f32[8,128]{1,0:T(8,128)S(1)}, f32[8,128]{1,0:T(8,128)S(1)}, u32[]{:S(2)}, u32[]{:S(2)}) collective-permute-start(f32[8,128]{1,0:T(8,128)S(1)} %power.1), channel_id=1, source_target_pairs={{0,8},{8,0},{16,24},{24,16},{1,9},{9,1},{17,25},{25,17},{2,10},{10... | collective-permute-start | bytes 12296 | tf_op jit(solution)/shard_map/ppermute | solution.py:225
  2.7 8.1 %collective-permute-start.1 = (f32[8,128]{1,0:T(8,128)S(1)}, f32[8,128]{1,0:T(8,128)S(1)}, u32[]{:S(2)}, u32[]{:S(2)}) collective-permute-start(f32[8,128]{1,0:T(8,128)S(1)} %power.1), channel_id=1, source_target_pairs={{0,16},{8,24},{16,0},{24,8},{1,17},{9,25},{17,1},{25,9},{2,18},{10... | collective-permute-start | bytes 12296 | tf_op jit(solution)/shard_map/ppermute | solution.py:225
  5.3 5.5 %collective-permute-start.2 = (f32[8,128]{1,0:T(8,128)S(1)}, f32[8,128]{1,0:T(8,128)S(1)}, u32[]{:S(2)}, u32[]{:S(2)}) collective-permute-start(f32[8,128]{1,0:T(8,128)S(1)} %power.1), channel_id=1, source_target_pairs={{0,24},{8,16},{16,8},{24,0},{1,25},{9,17},{17,9},{25,1},{2,26},{10... | collective-permute-start | bytes 12296 | tf_op jit(solution)/shard_map/ppermute | solution.py:225
  5.4 1.0 %copy-start.2 = (bf16[512,256]{1,0:T(8,128)(2,1)S(1)}, bf16[512,256]{1,0:T(8,128)(2,1)}, u32[]{:S(2)}) copy-start(bf16[512,256]{1,0:T(8,128)(2,1)} %constant.13.clone.band_ref) | copy-start | bytes 786436
  6.3 0.9 %copy-start.3 = (bf16[64,1024]{1,0:T(8,128)(2,1)S(1)}, bf16[64,1024]{1,0:T(8,128)(2,1)}, u32[]{:S(2)}) copy-start(bf16[64,1024]{1,0:T(8,128)(2,1)} %constant.14.clone.dft_ref) | copy-start | bytes 393220
  11.7 11.6 %all-to-all-start = ((bf16[8,80,128]{2,1,0:T(8,128)(2,1)}), bf16[8,80,128]{2,1,0:T(8,128)(2,1)S(1)}, u32[]{:S(2)}, u32[]{:S(2)}) async-start(bf16[8,80,128]{2,1,0:T(8,128)(2,1)} %broadcast_in_dim.7), calls=%async_computation | async-start | bytes 327680 | tf_op jit(solution)/shard_map/all_to_all | solution.py:238
  18.4 1.9 %collective-permute-start.3 = (bf16[4,16,128]{2,1,0:T(8,128)(2,1)S(1)}, bf16[4,16,128]{2,1,0:T(8,128)(2,1)S(1)}, u32[]{:S(2)}, u32[]{:S(2)}) collective-permute-start(bf16[4,16,128]{2,1,0:T(8,128)(2,1)S(1)} %spectra.1.own_ref), channel_id=1, source_target_pairs={{0,8},{8,0},{16,24},{24,16},{1,9},{9,1},{17,25},{25,17},{2,10},{10... | collective-permute-start | bytes 49160 | tf_op jit(solution)/shard_map/ppermute | solution.py:225
  18.4 3.7 %collective-permute-start.4 = (bf16[4,16,128]{2,1,0:T(8,128)(2,1)S(1)}, bf16[4,16,128]{2,1,0:T(8,128)(2,1)S(1)}, u32[]{:S(2)}, u32[]{:S(2)}) collective-permute-start(bf16[4,16,128]{2,1,0:T(8,128)(2,1)S(1)} %spectra.1.own_ref), channel_id=1, source_target_pairs={{0,16},{8,24},{16,0},{24,8},{1,17},{9,25},{17,1},{25,9},{2,18},{10... | collective-permute-start | bytes 49160 | tf_op jit(solution)/shard_map/ppermute | solution.py:225
  19.9 3.2 %collective-permute-start.5 = (bf16[4,16,128]{2,1,0:T(8,128)(2,1)S(1)}, bf16[4,16,128]{2,1,0:T(8,128)(2,1)S(1)}, u32[]{:S(2)}, u32[]{:S(2)}) collective-permute-start(bf16[4,16,128]{2,1,0:T(8,128)(2,1)S(1)} %spectra.1.own_ref), channel_id=1, source_target_pairs={{0,24},{8,16},{16,8},{24,0},{1,25},{9,17},{17,9},{25,1},{2,26},{10... | collective-permute-start | bytes 49160 | tf_op jit(solution)/shard_map/ppermute | solution.py:225

commit v2 on v1

v2 whole, which is shorter than its diff:
```python
import functools
import math

import jax
import jax.numpy as jnp
from jax import lax
from jax.experimental import pallas as pl
from jax.experimental.pallas import tpu as pltpu
from jax.sharding import PartitionSpec as P

W = 64
NS = 1024
HALF = 64
K0 = 6
FS = 4
SMOOTH = 4
BANDS = FS + 2 * SMOOTH
PAD = 16
TILE = 256
REACH = 128
LANES = 2 * W
POWER_ROWS = 16

BF16 = jnp.bfloat16
F32 = jnp.float32


def power_kernel(x_ref, out_ref):
    def add(channel, total):
        for tile in range(NS // 128):
            value = x_ref[channel, :, tile * 128 : (tile + 1) * 128].astype(F32)
            total = total + value * value
        return total

    total = lax.fori_loop(0, x_ref.shape[0], add, jnp.zeros((W, 128), F32))
    row = jnp.sum(jnp.transpose(total), axis=0, keepdims=True)
    out_ref[...] = jnp.broadcast_to(jnp.concatenate([row, row], axis=1), out_ref.shape)


def in_vmem(count):
    return [pl.BlockSpec(memory_space=pltpu.VMEM)] * count


def local_power(strain_rate):
    return pl.pallas_call(
        power_kernel,
        in_specs=in_vmem(1),
        out_specs=in_vmem(1)[0],
        out_shape=jax.ShapeDtypeStruct((8, LANES), F32),
        compiler_params=pltpu.CompilerParams(vmem_limit_bytes=4 * 2**20),
        name="power",
    )(strain_rate)


def whiten_rows(spectrum):
    real_part = spectrum[:BANDS]
    imag_part = spectrum[PAD : PAD + BANDS]
    magnitude = jnp.sqrt(real_part * real_part + imag_part * imag_part)
    smoothed = magnitude[0:FS]
    for offset in range(1, 2 * SMOOTH + 1):
        smoothed = smoothed + magnitude[offset : offset + FS]
    divisor = jnp.maximum(smoothed * (1.0 / (2 * SMOOTH + 1)), 0.6)
    return real_part[SMOOTH : SMOOTH + FS] / divisor, imag_part[SMOOTH : SMOOTH + FS] / divisor


def window_counts():
    sample = lax.broadcasted_iota(jnp.int32, (1, NS), 1)
    return (jnp.minimum(sample + HALF, NS - 1) - jnp.maximum(sample - HALF, 0) + 1).astype(F32)


def fill_band(band):
    source = lax.broadcasted_iota(jnp.int32, band.shape, 0) - REACH
    target = lax.broadcasted_iota(jnp.int32, band.shape, 1)
    band[...] = jnp.where(jnp.abs(source - target) <= HALF, 1.0, 0.0).astype(BF16)


def fill_dft(dft):
    bins = K0 + lax.broadcasted_iota(jnp.int32, (PAD, 128), 0)
    sample = lax.broadcasted_iota(jnp.int32, (PAD, 128), 1)
    turn = 2.0 * math.pi / NS
    phase = ((bins * sample) & (NS - 1)).astype(F32) * turn
    step = ((bins * 128) & (NS - 1)).astype(F32) * turn
    cos, sin = jnp.cos(phase), jnp.sin(phase)
    step_cos, step_sin = jnp.cos(step), jnp.sin(step)
    scale = window_counts() * (1.0 / math.sqrt(NS))
    for tile in range(NS // 128):
        place = slice(tile * 128, (tile + 1) * 128)
        for part, value in enumerate((cos * scale[:, place], -sin * scale[:, place])):
            high = value.astype(BF16)
            dft[part * PAD : (part + 1) * PAD, place] = high
            dft[(2 + part) * PAD : (3 + part) * PAD, place] = (value - high.astype(F32)).astype(BF16)
        cos, sin = cos * step_cos - sin * step_sin, sin * step_cos + cos * step_sin


def spectra_kernel(block, x_ref, out_ref, rows, band, dft):
    fill_band(band)
    fill_dft(dft)
    channels = x_ref.shape[0]
    small = window_counts() * 1e-06
    first_half = lax.broadcasted_iota(jnp.int32, (FS, LANES), 1) < W
    contract_samples = (((1,), (1,)), ((), ()))
    units = [
        (channel, tile) for channel in range(0, channels, block) for tile in range(NS // TILE)
    ]

    def running_sum(channel, tile):
        start, stop = tile * TILE, (tile + 1) * TILE
        low, high = max(start - REACH, 0), min(stop + REACH, NS)
        skip = low - (start - REACH)
        magnitude = jnp.abs(x_ref[channel : channel + block, :, low:high].reshape(-1, high - low))
        return jnp.dot(
            magnitude, band[skip : skip + high - low, :], preferred_element_type=F32
        )

    def flatten(channel, tile, running):
        start, stop = tile * TILE, (tile + 1) * TILE
        x = x_ref[channel : channel + block, :, start:stop].reshape(-1, TILE).astype(F32)
        flat = x / (running + small[:, start:stop])
        high = flat.astype(BF16)
        return high, (flat - high.astype(F32)).astype(BF16)

    def transform(tile, high, low):
        place = slice(tile * TILE, (tile + 1) * TILE)
        both = lax.dot_general(
            dft[:, place], high, contract_samples, preferred_element_type=F32
        )
        rest = lax.dot_general(
            dft[: 2 * PAD, place], low, contract_samples, preferred_element_type=F32
        )
        return both[: 2 * PAD] + (both[2 * PAD :] + rest)

    def store(channel, spectrum):
        white_real, white_imag = whiten_rows(spectrum)
        for pair in range(block // 2):
            real = white_real[:, pair * LANES : (pair + 1) * LANES]
            imag = white_imag[:, pair * LANES : (pair + 1) * LANES]
            even = jnp.where(first_half, real, pltpu.roll(imag, W, 1))
            odd = jnp.where(first_half, pltpu.roll(real, W, 1), imag)
            for bin_number in range(FS):
                for offset, value in enumerate((even, odd)):
                    row = channel + 2 * pair + offset
                    rows[bin_number, row : row + 1, :] = value[bin_number : bin_number + 1]

    spectrum = None
    running = running_sum(*units[0])
    for index, (channel, tile) in enumerate(units):
        following = running_sum(*units[index + 1]) if index + 1 < len(units) else None
        term = transform(tile, *flatten(channel, tile, running))
        spectrum = term if tile == 0 else spectrum + term
        if tile == NS // TILE - 1:
            store(channel, spectrum)
        running = following
    out_ref[...] = rows[...].astype(BF16)


def local_spectra(strain_rate, block=8):
    channels = strain_rate.shape[0]
    return pl.pallas_call(
        functools.partial(spectra_kernel, block),
        in_specs=in_vmem(1),
        out_specs=in_vmem(1)[0],
        out_shape=jax.ShapeDtypeStruct((FS, channels, LANES), BF16),
        scratch_shapes=[
            pltpu.VMEM((FS, channels, LANES), F32),
            pltpu.VMEM((TILE + 2 * REACH, TILE), BF16),
            pltpu.VMEM((4 * PAD, NS), BF16),
        ],
        compiler_params=pltpu.CompilerParams(vmem_limit_bytes=24 * 2**20),
        name="spectra",
    )(strain_rate)


def message_kernel(spectra_ref, own_ref, *refs):
    *power_refs, out_ref = refs
    rows = spectra_ref.shape[0] * spectra_ref.shape[1]
    power = own_ref[...]
    for ref in power_refs:
        power = power + ref[...]
    high = power.astype(BF16)
    rest = power - high.astype(F32)
    middle = rest.astype(BF16)
    low = (rest - middle.astype(F32)).astype(BF16)
    line = lax.broadcasted_iota(jnp.int32, power.shape, 0)
    parts = jnp.where(
        line == 0, high.astype(F32), jnp.where(line == 1, middle.astype(F32), low.astype(F32))
    )
    power_rows = jnp.concatenate([parts, parts], axis=0).astype(BF16)
    spectra = spectra_ref[...].reshape(rows, LANES)
    for receiver in range(out_ref.shape[0]):
        out_ref[receiver, :rows, :] = spectra
        out_ref[receiver, rows:, :] = power_rows


def cross_kernel(order, members, samples, me_ref, gathered_ref, own_ref, *refs):
    *row_refs, out_ref, first, second = refs
    channels = own_ref.shape[1]
    rows = FS * channels
    power = None
    for block in range(len(order)):
        parts = gathered_ref[block, rows : rows + POWER_ROWS, :].astype(F32)
        value = parts[0:1] + (parts[1:2] + parts[2:3])
        power = value if power is None else power + value
    power = power / (channels * members * samples)
    gain = 1.0 / jnp.sqrt(power + 1e-05)
    gain_square = gain * gain
    lane = lax.broadcasted_iota(jnp.int32, (1, LANES), 1)
    turned_gain = jnp.where(lane < W, -gain_square, gain_square)
    me = me_ref[0]
    for shift, ref in enumerate((own_ref, *row_refs)):
        row = jnp.bitwise_xor(me, shift)
        place = pl.ds(pl.multiple_of(row * channels, channels), channels)
        for bin_number in range(FS):
            value = ref[bin_number].astype(F32)
            second[0, bin_number, place, :] = (value * gain_square).astype(BF16)
            second[1, bin_number, place, :] = (pltpu.roll(value, W, 1) * turned_gain).astype(BF16)
    for block, column in enumerate(order):
        for bin_number in range(FS):
            first[bin_number, column * channels : (column + 1) * channels, :] = gathered_ref[
                block, bin_number * channels : (bin_number + 1) * channels, :
            ]
    for bin_number in range(FS):
        for part in range(2):
            total = lax.dot_general(
                second[part, bin_number],
                first[bin_number],
                (((1,), (1,)), ((), ())),
                preferred_element_type=F32,
            )
            out_ref[part, bin_number] = (total * (1.0 / W)).astype(BF16)


def column_order(col_count):
    best = [4, 0, 5, 6, 1, 2, 7, 3]
    if col_count == len(best):
        return best
    middle = col_count // 2
    return [middle, *(c for c in range(col_count) if c != middle)]


def shards(strain_rate):
    channels, windows, samples = strain_rate.shape
    row_count = lax.axis_size("row")
    col_count = lax.axis_size("col")
    order = column_order(col_count)

    def from_row(value, shift):
        return lax.ppermute(value, "row", [(i, i ^ shift) for i in range(row_count)])

    own_power = local_power(strain_rate)
    powers = [from_row(own_power, shift) for shift in range(1, row_count)]
    spectra = local_spectra(strain_rate)
    message = pl.pallas_call(
        message_kernel,
        in_specs=in_vmem(1 + row_count),
        out_specs=in_vmem(1)[0],
        out_shape=jax.ShapeDtypeStruct((col_count, FS * channels + POWER_ROWS, LANES), BF16),
        compiler_params=pltpu.CompilerParams(vmem_limit_bytes=8 * 2**20),
        name="message",
    )(spectra, own_power, *powers)
    gathered = lax.all_to_all(message, "col", 0, 0, axis_index_groups=[order])
    others = [from_row(spectra, shift) for shift in range(1, row_count)]
    me = lax.axis_index("row").astype(jnp.int32).reshape(1)
    result = pl.pallas_call(
        functools.partial(cross_kernel, order, row_count * col_count, samples),
        in_specs=[pl.BlockSpec(memory_space=pltpu.SMEM)]
        + [pl.BlockSpec(memory_space=pltpu.VMEM)] * (2 + len(others)),
        out_specs=pl.BlockSpec(memory_space=pltpu.VMEM),
        out_shape=jax.ShapeDtypeStruct(
            (2, FS, row_count * channels, col_count * channels), BF16
        ),
        scratch_shapes=[
            pltpu.VMEM((FS, col_count * channels, LANES), BF16),
            pltpu.VMEM((2, FS, row_count * channels, LANES), BF16),
        ],
        compiler_params=pltpu.CompilerParams(vmem_limit_bytes=8 * 2**20),
        name="cross",
    )(me, gathered, spectra, *others)
    return result.reshape(2, FS, 1, row_count, channels, -1)


def solution(mesh):
    return jax.shard_map(
        shards,
        mesh=mesh,
        in_specs=(P(("row", "col"), None, None),),
        out_specs=P(None, None, "col", None, None, "row"),
        check_vma=False,
    )
```

time: 24.6 us -> 21.7 us (0.88)
  local copies, waits for them, and re-layouts: 4.31 us -> 1.59 us
    unnamed x10 -> x4, local copies, waits for them, and re-layouts: 3.45 us -> 1.59 us
    broadcast_in_dim x2 -> x0, local copies, waits for them, and re-layouts: 0.69 us -> none  [the longest x1 0.69 us: shards(): jnp.broadcast_to(message, (col_count, *message.shape))]
    pallas_call x2 -> x3, Pallas kernels: 4.23 us -> 4.11 us  [the longest x1 2.8 us: local_spectra(): pl.pallas_call(functools.partial(spectra_kernel, block), in_specs=in_vmem...]
  transfers between devices with their start and end apart: 7 -> 7, of which waited for: 3 -> 4; matrix products, arithmetic and copies ran while one was open for 0% -> 0% of each run, Pallas kernels for 15% -> 13%
where the time goes in v2:
time: 21.7 us; the launch traced here: 21.4 us
  starting transfers between devices  11.5 us (53%)
  Pallas kernels  5.12 us (24%)
  waiting for transfers between devices  3.23 us (15%)
  local copies, waits for them, and re-layouts  1.59 us (7%)
    all_to_all x1, starting transfers between devices, shards(): gathered = lax.all_to_all(message, 'col', 0, 0, axis_index_groups=[order])  6.51 us
    ppermute x6, starting transfers between devices, from_row(): lax.ppermute(value, 'row', [(i, i ^ shift) for i in range(row_count)])  4.95 us
    ppermute x6, waiting for transfers between devices, from_row(): lax.ppermute(value, 'row', [(i, i ^ shift) for i in range(row_count)])  2.93 us
    pallas_call x1, Pallas kernels, local_spectra(): pl.pallas_call(functools.partial(spectra_kernel, block), in_specs=in_vmem...  2.8 us
    unnamed x4, local copies, waits for them, and re-layouts  1.59 us
    pallas_call x1, Pallas kernels, shards(): pl.pallas_call(functools.partial(cross_kernel, order, row_count * col_cou...  1.01 us
    pallas_call x1, Pallas kernels, shards(): pl.pallas_call(message_kernel, in_specs=in_vmem(1 + row_count), out_specs...  0.68 us
    pallas_call x1, Pallas kernels, local_power(): pl.pallas_call(power_kernel, in_specs=in_vmem(1), out_specs=in_vmem(1)[0]...  0.63 us
  transfers between devices with their start and end apart: 7, of which 4 were waited for; matrix products, arithmetic and copies ran while one was open for 0% of the time, Pallas kernels for 13%

profile of v2, /device:TPU:0, one launch (start us, length us, event | category | flops | bytes accessed | tf_op | source)
XLA Modules:
  0.0 21.4 jit_solution(16074139172079307320)
XLA Ops:
  0.0 0.0 copy-start
  0.0 1.6 %copy-done = bf16[16,64,1024]{2,1,0:T(8,128)(2,1)S(1)} copy-done((bf16[16,64,1024]{2,1,0:T(8,128)(2,1)S(1)}, bf16[16,64,1024]{2,1,0:T(8,128)(2,1)}, u32[]{:S(2)}) %copy-start) | copy-done | bytes 2097176
  1.6 0.0 copy-start.1
  1.6 0.6 %power.1.own_ref = f32[8,128]{1,0:T(8,128)S(1)} custom-call(bf16[16,64,1024]{2,1,0:T(8,128)(2,1)S(1)} %copy-done), custom_call_target="tpu_custom_call" | custom-call | tf_op jit(solution)/shard_map/power/pallas_call | solution.py:45
  2.2 0.5 %collective-permute-start = (f32[8,128]{1,0:T(8,128)S(1)}, f32[8,128]{1,0:T(8,128)S(1)}, u32[]{:S(2)}, u32[]{:S(2)}) collective-permute-start(f32[8,128]{1,0:T(8,128)S(1)} %power.1.own_ref), channel_id=1, source_target_pairs={{0,8},{8,0},{16,24},{24,16},{1,9},{9,1},{17,25},{25,17},{2,10},{10... | collective-permute-start | bytes 12296 | tf_op jit(solution)/shard_map/ppermute | solution.py:247
  2.7 2.6 %collective-permute-start.1 = (f32[8,128]{1,0:T(8,128)S(1)}, f32[8,128]{1,0:T(8,128)S(1)}, u32[]{:S(2)}, u32[]{:S(2)}) collective-permute-start(f32[8,128]{1,0:T(8,128)S(1)} %power.1.own_ref), channel_id=1, source_target_pairs={{0,16},{8,24},{16,0},{24,8},{1,17},{9,25},{17,1},{25,9},{2,18},{10... | collective-permute-start | bytes 12296 | tf_op jit(solution)/shard_map/ppermute | solution.py:247
  5.2 0.1 collective-permute-start.2
  5.3 0.0 copy-done.1
  5.3 2.8 %spectra.1.spectra_ref.own_ref = bf16[4,16,128]{2,1,0:T(8,128)(2,1)S(1)} custom-call(bf16[16,64,1024]{2,1,0:T(8,128)(2,1)S(1)} %copy-done.1), custom_call_target="tpu_custom_call" | custom-call | tf_op jit(solution)/shard_map/spectra/pallas_call | solution.py:158
  8.1 0.0 collective-permute-done.refs_0_
  8.1 0.0 collective-permute-done.1.refs_1_
  8.1 0.1 collective-permute-done.2.refs_2_
  8.3 0.7 %message.1 = bf16[8,80,128]{2,1,0:T(8,128)(2,1)} custom-call(bf16[4,16,128]{2,1,0:T(8,128)(2,1)S(1)} %spectra.1.spectra_ref.own_ref, f32[8,128]{1,0:T(8,128)S(1)} %power.1.own_ref, f32[8,128]{1,0:T(8,128)S(1)} %collective-permute-done.refs_0_, f32[8,128]{1,0:T(8,128)S(1)} %collective-permute-done.1.refs_1_, f32[8,128]{1,0:T(8,128)S(1)} %collective-permute-done.2.refs_2_), custom_call_target="tpu_custom_call" | custom-call | tf_op jit(solution)/shard_map/message/pallas_call | solution.py:252
  9.0 6.5 %all-to-all-start = ((bf16[8,80,128]{2,1,0:T(8,128)(2,1)}), bf16[8,80,128]{2,1,0:T(8,128)(2,1)S(1)}, u32[]{:S(2)}, u32[]{:S(2)}) async-start(bf16[8,80,128]{2,1,0:T(8,128)(2,1)} %message.1), calls=%async_computation | async-start | bytes 327680 | tf_op jit(solution)/shard_map/all_to_all | solution.py:260
  15.5 0.0 collective-permute-start.3
  15.5 1.5 %collective-permute-start.4 = (bf16[4,16,128]{2,1,0:T(8,128)(2,1)S(1)}, bf16[4,16,128]{2,1,0:T(8,128)(2,1)S(1)}, u32[]{:S(2)}, u32[]{:S(2)}) collective-permute-start(bf16[4,16,128]{2,1,0:T(8,128)(2,1)S(1)} %spectra.1.spectra_ref.own_ref), channel_id=1, source_target_pairs={{0,16},{8,24},{16,0},{24,8},{1,17},{9,25},{17,1},{25,9},{2,18},{10... | collective-permute-start | bytes 49160 | tf_op jit(solution)/shard_map/ppermute | solution.py:247
  17.0 0.4 %collective-permute-start.5 = (bf16[4,16,128]{2,1,0:T(8,128)(2,1)S(1)}, bf16[4,16,128]{2,1,0:T(8,128)(2,1)S(1)}, u32[]{:S(2)}, u32[]{:S(2)}) collective-permute-start(bf16[4,16,128]{2,1,0:T(8,128)(2,1)S(1)} %spectra.1.spectra_ref.own_ref), channel_id=1, source_target_pairs={{0,24},{8,16},{16,8},{24,0},{1,25},{9,17},{17,9},{25,1},{2,26},{10... | collective-permute-start | bytes 49160 | tf_op jit(solution)/shard_map/ppermute | solution.py:247
  17.3 0.0 collective-permute-done.3.refs_0_
  17.3 1.9 %collective-permute-done.4.refs_1_ = bf16[4,16,128]{2,1,0:T(8,128)(2,1)S(1)} collective-permute-done((bf16[4,16,128]{2,1,0:T(8,128)(2,1)S(1)}, bf16[4,16,128]{2,1,0:T(8,128)(2,1)S(1)}, u32[]{:S(2)}, u32[]{:S(2)}) %collective-permute-start.4) | collective-permute-done | bytes 16416 | tf_op jit(solution)/shard_map/ppermute | solution.py:247
  19.2 0.9 %collective-permute-done.5.refs_2_ = bf16[4,16,128]{2,1,0:T(8,128)(2,1)S(1)} collective-permute-done((bf16[4,16,128]{2,1,0:T(8,128)(2,1)S(1)}, bf16[4,16,128]{2,1,0:T(8,128)(2,1)S(1)}, u32[]{:S(2)}, u32[]{:S(2)}) %collective-permute-start.5) | collective-permute-done | bytes 16416 | tf_op jit(solution)/shard_map/ppermute | solution.py:247
  20.1 0.3 %all-to-all-done.gathered_ref = bf16[8,80,128]{2,1,0:T(8,128)(2,1)S(1)} async-done(((bf16[8,80,128]{2,1,0:T(8,128)(2,1)}), bf16[8,80,128]{2,1,0:T(8,128)(2,1)S(1)}, u32[]{:S(2)}, u32[]{:S(2)}) %all-to-all-start) | async-done | bytes 163872 | tf_op jit(solution)/shard_map/all_to_all | solution.py:260
  20.4 1.0 %cross.1 = bf16[2,4,64,128]{3,2,1,0:T(8,128)(2,1)} custom-call(s32[1]{0:T(128)} %bitcast.me_ref, bf16[8,80,128]{2,1,0:T(8,128)(2,1)S(1)} %all-to-all-done.gathered_ref, bf16[4,16,128]{2,1,0:T(8,128)(2,1)S(1)} %spectra.1.spectra_ref.own_ref, bf16[4,16,128]{2,1,0:T(8,128)(2,1)S(1)} %collective-permute-done.3.refs_0_, ...), custom_call_target="tpu_custom_call" | custom-call | tf_op jit(solution)/shard_map/cross/pallas_call | solution.py:263
Async XLA Ops:
  0.0 1.6 %copy-start = (bf16[16,64,1024]{2,1,0:T(8,128)(2,1)S(1)}, bf16[16,64,1024]{2,1,0:T(8,128)(2,1)}, u32[]{:S(2)}) copy-start(bf16[16,64,1024]{2,1,0:T(8,128)(2,1)} %x_ref.3) | copy-start | bytes 6291460
  1.6 3.7 %copy-start.1 = (bf16[16,64,1024]{2,1,0:T(8,128)(2,1)S(1)}, bf16[16,64,1024]{2,1,0:T(8,128)(2,1)}, u32[]{:S(2)}) copy-start(bf16[16,64,1024]{2,1,0:T(8,128)(2,1)} %x_ref.3) | copy-start | bytes 6291460
  2.2 5.9 %collective-permute-start = (f32[8,128]{1,0:T(8,128)S(1)}, f32[8,128]{1,0:T(8,128)S(1)}, u32[]{:S(2)}, u32[]{:S(2)}) collective-permute-start(f32[8,128]{1,0:T(8,128)S(1)} %power.1.own_ref), channel_id=1, source_target_pairs={{0,8},{8,0},{16,24},{24,16},{1,9},{9,1},{17,25},{25,17},{2,10},{10... | collective-permute-start | bytes 12296 | tf_op jit(solution)/shard_map/ppermute | solution.py:247
  2.7 5.5 %collective-permute-start.1 = (f32[8,128]{1,0:T(8,128)S(1)}, f32[8,128]{1,0:T(8,128)S(1)}, u32[]{:S(2)}, u32[]{:S(2)}) collective-permute-start(f32[8,128]{1,0:T(8,128)S(1)} %power.1.own_ref), channel_id=1, source_target_pairs={{0,16},{8,24},{16,0},{24,8},{1,17},{9,25},{17,1},{25,9},{2,18},{10... | collective-permute-start | bytes 12296 | tf_op jit(solution)/shard_map/ppermute | solution.py:247
  5.2 3.0 %collective-permute-start.2 = (f32[8,128]{1,0:T(8,128)S(1)}, f32[8,128]{1,0:T(8,128)S(1)}, u32[]{:S(2)}, u32[]{:S(2)}) collective-permute-start(f32[8,128]{1,0:T(8,128)S(1)} %power.1.own_ref), channel_id=1, source_target_pairs={{0,24},{8,16},{16,8},{24,0},{1,25},{9,17},{17,9},{25,1},{2,26},{10... | collective-permute-start | bytes 12296 | tf_op jit(solution)/shard_map/ppermute | solution.py:247
  9.0 11.5 %all-to-all-start = ((bf16[8,80,128]{2,1,0:T(8,128)(2,1)}), bf16[8,80,128]{2,1,0:T(8,128)(2,1)S(1)}, u32[]{:S(2)}, u32[]{:S(2)}) async-start(bf16[8,80,128]{2,1,0:T(8,128)(2,1)} %message.1), calls=%async_computation | async-start | bytes 327680 | tf_op jit(solution)/shard_map/all_to_all | solution.py:260
  15.5 1.9 %collective-permute-start.3 = (bf16[4,16,128]{2,1,0:T(8,128)(2,1)S(1)}, bf16[4,16,128]{2,1,0:T(8,128)(2,1)S(1)}, u32[]{:S(2)}, u32[]{:S(2)}) collective-permute-start(bf16[4,16,128]{2,1,0:T(8,128)(2,1)S(1)} %spectra.1.spectra_ref.own_ref), channel_id=1, source_target_pairs={{0,8},{8,0},{16,24},{24,16},{1,9},{9,1},{17,25},{25,17},{2,10},{10... | collective-permute-start | bytes 49160 | tf_op jit(solution)/shard_map/ppermute | solution.py:247
  15.5 3.7 %collective-permute-start.4 = (bf16[4,16,128]{2,1,0:T(8,128)(2,1)S(1)}, bf16[4,16,128]{2,1,0:T(8,128)(2,1)S(1)}, u32[]{:S(2)}, u32[]{:S(2)}) collective-permute-start(bf16[4,16,128]{2,1,0:T(8,128)(2,1)S(1)} %spectra.1.spectra_ref.own_ref), channel_id=1, source_target_pairs={{0,16},{8,24},{16,0},{24,8},{1,17},{9,25},{17,1},{25,9},{2,18},{10... | collective-permute-start | bytes 49160 | tf_op jit(solution)/shard_map/ppermute | solution.py:247
  17.0 3.2 %collective-permute-start.5 = (bf16[4,16,128]{2,1,0:T(8,128)(2,1)S(1)}, bf16[4,16,128]{2,1,0:T(8,128)(2,1)S(1)}, u32[]{:S(2)}, u32[]{:S(2)}) collective-permute-start(bf16[4,16,128]{2,1,0:T(8,128)(2,1)S(1)} %spectra.1.spectra_ref.own_ref), channel_id=1, source_target_pairs={{0,24},{8,16},{16,8},{24,0},{1,25},{9,17},{17,9},{25,1},{2,26},{10... | collective-permute-start | bytes 49160 | tf_op jit(solution)/shard_map/ppermute | solution.py:247

commit v3 on v2

--- a/solution.py
+++ b/solution.py
@@ -25,31 +25,8 @@
 F32 = jnp.float32
 
 
-def power_kernel(x_ref, out_ref):
-    def add(channel, total):
-        for tile in range(NS // 128):
-            value = x_ref[channel, :, tile * 128 : (tile + 1) * 128].astype(F32)
-            total = total + value * value
-        return total
-
-    total = lax.fori_loop(0, x_ref.shape[0], add, jnp.zeros((W, 128), F32))
-    row = jnp.sum(jnp.transpose(total), axis=0, keepdims=True)
-    out_ref[...] = jnp.broadcast_to(jnp.concatenate([row, row], axis=1), out_ref.shape)
-
-
 def in_vmem(count):
     return [pl.BlockSpec(memory_space=pltpu.VMEM)] * count
-
-
-def local_power(strain_rate):
-    return pl.pallas_call(
-        power_kernel,
-        in_specs=in_vmem(1),
-        out_specs=in_vmem(1)[0],
-        out_shape=jax.ShapeDtypeStruct((8, LANES), F32),
-        compiler_params=pltpu.CompilerParams(vmem_limit_bytes=4 * 2**20),
-        name="power",
-    )(strain_rate)
 
 
 def whiten_rows(spectrum):
@@ -92,9 +69,48 @@
         cos, sin = cos * step_cos - sin * step_sin, sin * step_cos + cos * step_sin
 
 
-def spectra_kernel(block, x_ref, out_ref, rows, band, dft):
+def front_kernel(x_hbm, x_ref, power_ref, band, dft, arrived):
+    parts = arrived.shape[0]
+    size = x_hbm.shape[0] // parts
+    copies = [
+        pltpu.make_async_copy(
+            x_hbm.at[pl.ds(part * size, size)], x_ref.at[pl.ds(part * size, size)], arrived.at[part]
+        )
+        for part in range(parts)
+    ]
+    for copy in copies:
+        copy.start()
     fill_band(band)
     fill_dft(dft)
+    total = jnp.zeros((W, 128), F32)
+    for part, copy in enumerate(copies):
+        copy.wait()
+        for channel in range(part * size, (part + 1) * size):
+            for tile in range(NS // 128):
+                value = x_ref[channel, :, tile * 128 : (tile + 1) * 128].astype(F32)
+                total = total + value * value
+    row = jnp.sum(jnp.transpose(total), axis=0, keepdims=True)
+    power_ref[...] = jnp.broadcast_to(jnp.concatenate([row, row], axis=1), power_ref.shape)
+
+
+def front(strain_rate, parts=8):
+    return pl.pallas_call(
+        front_kernel,
+        in_specs=[pl.BlockSpec(memory_space=pltpu.HBM)],
+        out_specs=in_vmem(4),
+        out_shape=[
+            jax.ShapeDtypeStruct(strain_rate.shape, BF16),
+            jax.ShapeDtypeStruct((8, LANES), F32),
+            jax.ShapeDtypeStruct((TILE + 2 * REACH, TILE), BF16),
+            jax.ShapeDtypeStruct((4 * PAD, NS), BF16),
+        ],
+        scratch_shapes=[pltpu.SemaphoreType.DMA((math.gcd(parts, strain_rate.shape[0]),))],
+        compiler_params=pltpu.CompilerParams(vmem_limit_bytes=51 * 2**20),
+        name="front",
+    )(strain_rate)
+
+
+def spectra_kernel(block, x_ref, band, dft, out_ref, rows):
     channels = x_ref.shape[0]
     small = window_counts() * 1e-06
     first_half = lax.broadcasted_iota(jnp.int32, (FS, LANES), 1) < W
@@ -141,33 +157,32 @@
                     row = channel + 2 * pair + offset
                     rows[bin_number, row : row + 1, :] = value[bin_number : bin_number + 1]
 
-    spectrum = None
-    running = running_sum(*units[0])
-    for index, (channel, tile) in enumerate(units):
-        following = running_sum(*units[index + 1]) if index + 1 < len(units) else None
-        term = transform(tile, *flatten(channel, tile, running))
-        spectrum = term if tile == 0 else spectrum + term
-        if tile == NS // TILE - 1:
-            store(channel, spectrum)
-        running = following
+    summed, flattened = {}, {}
+    for index in range(len(units) + 2):
+        if index < len(units):
+            summed[index] = running_sum(*units[index])
+        if 1 <= index <= len(units):
+            flattened[index - 1] = flatten(*units[index - 1], summed.pop(index - 1))
+        if index >= 2:
+            channel, tile = units[index - 2]
+            term = transform(tile, *flattened.pop(index - 2))
+            spectrum = term if tile == 0 else spectrum + term
+            if tile == NS // TILE - 1:
+                store(channel, spectrum)
     out_ref[...] = rows[...].astype(BF16)
 
 
-def local_spectra(strain_rate, block=8):
+def local_spectra(strain_rate, band, dft, block=8):
     channels = strain_rate.shape[0]
     return pl.pallas_call(
         functools.partial(spectra_kernel, block),
-        in_specs=in_vmem(1),
+        in_specs=in_vmem(3),
         out_specs=in_vmem(1)[0],
         out_shape=jax.ShapeDtypeStruct((FS, channels, LANES), BF16),
-        scratch_shapes=[
-            pltpu.VMEM((FS, channels, LANES), F32),
-            pltpu.VMEM((TILE + 2 * REACH, TILE), BF16),
-            pltpu.VMEM((4 * PAD, NS), BF16),
-        ],
+        scratch_shapes=[pltpu.VMEM((FS, channels, LANES), F32)],
         compiler_params=pltpu.CompilerParams(vmem_limit_bytes=24 * 2**20),
         name="spectra",
-    )(strain_rate)
+    )(strain_rate, band, dft)
 
 
 def message_kernel(spectra_ref, own_ref, *refs):
@@ -191,8 +206,8 @@
         out_ref[receiver, rows:, :] = power_rows
 
 
-def cross_kernel(order, members, samples, me_ref, gathered_ref, own_ref, *refs):
-    *row_refs, out_ref, first, second = refs
+def cross_kernel(order, members, samples, gathered_ref, own_ref, *refs):
+    *row_refs, out_hbm, second, out_ref, sent = refs
     channels = own_ref.shape[1]
     rows = FS * channels
     power = None
@@ -205,32 +220,40 @@
     gain_square = gain * gain
     lane = lax.broadcasted_iota(jnp.int32, (1, LANES), 1)
     turned_gain = jnp.where(lane < W, -gain_square, gain_square)
-    me = me_ref[0]
-    for shift, ref in enumerate((own_ref, *row_refs)):
-        row = jnp.bitwise_xor(me, shift)
-        place = pl.ds(pl.multiple_of(row * channels, channels), channels)
-        for bin_number in range(FS):
+    me = lax.axis_index("row")
+    copies = []
+    for bin_number in range(FS):
+        for shift, ref in enumerate((own_ref, *row_refs)):
+            row = jnp.bitwise_xor(me, shift)
+            place = pl.ds(pl.multiple_of(row * channels, channels), channels)
             value = ref[bin_number].astype(F32)
-            second[0, bin_number, place, :] = (value * gain_square).astype(BF16)
-            second[1, bin_number, place, :] = (pltpu.roll(value, W, 1) * turned_gain).astype(BF16)
-    for block, column in enumerate(order):
-        for bin_number in range(FS):
-            first[bin_number, column * channels : (column + 1) * channels, :] = gathered_ref[
-                block, bin_number * channels : (bin_number + 1) * channels, :
-            ]
-    for bin_number in range(FS):
-        for part in range(2):
-            total = lax.dot_general(
-                second[part, bin_number],
-                first[bin_number],
-                (((1,), (1,)), ((), ())),
-                preferred_element_type=F32,
-            )
-            out_ref[part, bin_number] = (total * (1.0 / W)).astype(BF16)
+            second[bin_number, 0, place, :] = (value * gain_square).astype(BF16)
+            second[bin_number, 1, place, :] = (pltpu.roll(value, W, 1) * turned_gain).astype(BF16)
+        first = jnp.concatenate(
+            [
+                gathered_ref[order.index(column), bin_number * channels : (bin_number + 1) * channels, :]
+                for column in range(len(order))
+            ],
+            axis=0,
+        )
+        total = lax.dot_general(
+            second[bin_number].reshape(-1, LANES),
+            first,
+            (((1,), (1,)), ((), ())),
+            preferred_element_type=F32,
+        )
+        out_ref[bin_number] = (total * (1.0 / W)).astype(BF16).reshape(out_ref.shape[1:])
+        copy = pltpu.make_async_copy(
+            out_ref.at[bin_number], out_hbm.at[:, bin_number], sent.at[bin_number]
+        )
+        copy.start()
+        copies.append(copy)
+    for copy in copies:
+        copy.wait()
 
 
 def column_order(col_count):
-    best = [4, 0, 5, 6, 1, 2, 7, 3]
+    best = [4, 2, 6, 5, 1, 0, 7, 3]
     if col_count == len(best):
         return best
     middle = col_count // 2
@@ -246,9 +269,9 @@
     def from_row(value, shift):
         return lax.ppermute(value, "row", [(i, i ^ shift) for i in range(row_count)])
 
-    own_power = local_power(strain_rate)
+    held, own_power, band, dft = front(strain_rate)
     powers = [from_row(own_power, shift) for shift in range(1, row_count)]
-    spectra = local_spectra(strain_rate)
+    spectra = local_spectra(held, band, dft)
     message = pl.pallas_call(
         message_kernel,
         in_specs=in_vmem(1 + row_count),
@@ -259,22 +282,21 @@
     )(spectra, own_power, *powers)
     gathered = lax.all_to_all(message, "col", 0, 0, axis_index_groups=[order])
     others = [from_row(spectra, shift) for shift in range(1, row_count)]
-    me = lax.axis_index("row").astype(jnp.int32).reshape(1)
     result = pl.pallas_call(
         functools.partial(cross_kernel, order, row_count * col_count, samples),
-        in_specs=[pl.BlockSpec(memory_space=pltpu.SMEM)]
-        + [pl.BlockSpec(memory_space=pltpu.VMEM)] * (2 + len(others)),
-        out_specs=pl.BlockSpec(memory_space=pltpu.VMEM),
+        in_specs=in_vmem(2 + len(others)),
+        out_specs=pl.BlockSpec(memory_space=pltpu.HBM),
         out_shape=jax.ShapeDtypeStruct(
             (2, FS, row_count * channels, col_count * channels), BF16
         ),
         scratch_shapes=[
-            pltpu.VMEM((FS, col_count * channels, LANES), BF16),
-            pltpu.VMEM((2, FS, row_count * channels, LANES), BF16),
+            pltpu.VMEM((FS, 2, row_count * channels, LANES), BF16),
+            pltpu.VMEM((FS, 2, row_count * channels, col_count * channels), BF16),
+            pltpu.SemaphoreType.DMA((FS,)),
         ],
         compiler_params=pltpu.CompilerParams(vmem_limit_bytes=8 * 2**20),
         name="cross",
-    )(me, gathered, spectra, *others)
+    )(gathered, spectra, *others)
     return result.reshape(2, FS, 1, row_count, channels, -1)
 
 

time: 21.7 us -> 20.6 us (0.949)
  local copies, waits for them, and re-layouts: 1.59 us -> 0 us
  Pallas kernels: 5.12 us -> 5.93 us
    unnamed x4 -> x0, local copies, waits for them, and re-layouts: 1.59 us -> none
    pallas_call x1, Pallas kernels: 0.63 us -> 1.79 us  [front(): pl.pallas_call(front_kernel, in_specs=[pl.BlockSpec(memory_space=pltpu.HB...]
    pallas_call x1, Pallas kernels: 2.8 us -> 2.53 us  [local_spectra(): pl.pallas_call(functools.partial(spectra_kernel, block), in_specs=in_vmem...]
    all_to_all x1, waiting for transfers between devices: 0.3 us -> 0.05 us  [shards(): gathered = lax.all_to_all(message, 'col', 0, 0, axis_index_groups=[order])]
  transfers between devices with their start and end apart: 7 -> 7, of which waited for: 4 -> 4; matrix products, arithmetic and copies ran while one was open for 0% -> 0% of each run, Pallas kernels for 13% -> 12%
where the time goes in v3:
time: 20.6 us; the launch traced here: 20.4 us
  starting transfers between devices  11.4 us (55%)
  Pallas kernels  5.93 us (29%)
  waiting for transfers between devices  3.02 us (15%)
    all_to_all x1, starting transfers between devices, shards(): gathered = lax.all_to_all(message, 'col', 0, 0, axis_index_groups=[order])  6.39 us
    ppermute x6, starting transfers between devices, from_row(): lax.ppermute(value, 'row', [(i, i ^ shift) for i in range(row_count)])  4.98 us
    ppermute x6, waiting for transfers between devices, from_row(): lax.ppermute(value, 'row', [(i, i ^ shift) for i in range(row_count)])  2.97 us
    pallas_call x1, Pallas kernels, local_spectra(): pl.pallas_call(functools.partial(spectra_kernel, block), in_specs=in_vmem...  2.53 us
    pallas_call x1, Pallas kernels, front(): pl.pallas_call(front_kernel, in_specs=[pl.BlockSpec(memory_space=pltpu.HB...  1.79 us
    pallas_call x1, Pallas kernels, shards(): pl.pallas_call(functools.partial(cross_kernel, order, row_count * col_cou...  0.92 us
    pallas_call x1, Pallas kernels, shards(): pl.pallas_call(message_kernel, in_specs=in_vmem(1 + row_count), out_specs...  0.68 us
  transfers between devices with their start and end apart: 7, of which 4 were waited for; matrix products, arithmetic and copies ran while one was open for 0% of the time, Pallas kernels for 12%

profile of v3, /device:TPU:0, one launch (start us, length us, event | category | flops | bytes accessed | tf_op | source)
XLA Modules:
  0.0 20.4 jit_solution(7526412118922404588)
XLA Ops:
  0.0 1.8 %front.1 = (bf16[16,64,1024]{2,1,0:T(8,128)(2,1)S(1)}, f32[8,128]{1,0:T(8,128)S(1)}, bf16[512,256]{1,0:T(8,128)(2,1)S(1)}, bf16[64,1024]{1,0:T(8,128)(2,1)S(1)}) custom-call(bf16[16,64,1024]{2,1,0:T(8,128)(2,1)} %x_hbm.1), custom_call_target="tpu_custom_call" | custom-call | tf_op jit(solution)/shard_map/front/pallas_call | solution.py:97
  1.8 2.4 %collective-permute-start.2 = (f32[8,128]{1,0:T(8,128)S(1)}, f32[8,128]{1,0:T(8,128)S(1)}, u32[]{:S(2)}, u32[]{:S(2)}) collective-permute-start(f32[8,128]{1,0:T(8,128)S(1)} %get-tuple-element.12.own_ref), channel_id=1, source_target_pairs={{0,24},{8,16},{16,8},{24,0},{1,25},{9,17},{17,9},{25,1},{2,26},{10... | collective-permute-start | bytes 12296 | tf_op jit(solution)/shard_map/ppermute | solution.py:270
  4.2 0.6 %collective-permute-start.1 = (f32[8,128]{1,0:T(8,128)S(1)}, f32[8,128]{1,0:T(8,128)S(1)}, u32[]{:S(2)}, u32[]{:S(2)}) collective-permute-start(f32[8,128]{1,0:T(8,128)S(1)} %get-tuple-element.12.own_ref), channel_id=1, source_target_pairs={{0,16},{8,24},{16,0},{24,8},{1,17},{9,25},{17,1},{25,9},{2,18},{10... | collective-permute-start | bytes 12296 | tf_op jit(solution)/shard_map/ppermute | solution.py:270
  4.9 0.0 collective-permute-start
  4.9 2.5 %spectra.1.spectra_ref.own_ref = bf16[4,16,128]{2,1,0:T(8,128)(2,1)S(1)} custom-call(bf16[16,64,1024]{2,1,0:T(8,128)(2,1)S(1)} %get-tuple-element.9.x_ref, bf16[512,256]{1,0:T(8,128)(2,1)S(1)} %get-tuple-element.10.band, bf16[64,1024]{1,0:T(8,128)(2,1)S(1)} %get-tuple-element.11.dft), custom_call_target="tpu_custom_call" | custom-call | tf_op jit(solution)/shard_map/spectra/pallas_call | solution.py:177
  7.5 0.0 collective-permute-done.2.refs_2_
  7.5 0.4 %collective-permute-done.1.refs_1_ = f32[8,128]{1,0:T(8,128)S(1)} collective-permute-done((f32[8,128]{1,0:T(8,128)S(1)}, f32[8,128]{1,0:T(8,128)S(1)}, u32[]{:S(2)}, u32[]{:S(2)}) %collective-permute-start.1) | collective-permute-done | bytes 4128 | tf_op jit(solution)/shard_map/ppermute | solution.py:270
  7.9 0.0 collective-permute-done.refs_0_
  7.9 0.7 %message.1 = bf16[8,80,128]{2,1,0:T(8,128)(2,1)} custom-call(bf16[4,16,128]{2,1,0:T(8,128)(2,1)S(1)} %spectra.1.spectra_ref.own_ref, f32[8,128]{1,0:T(8,128)S(1)} %get-tuple-element.12.own_ref, f32[8,128]{1,0:T(8,128)S(1)} %collective-permute-done.refs_0_, f32[8,128]{1,0:T(8,128)S(1)} %collective-permute-done.1.refs_1_, ...), custom_call_target="tpu_custom_call" | custom-call | tf_op jit(solution)/shard_map/message/pallas_call | solution.py:275
  8.5 6.4 %all-to-all-start = ((bf16[8,80,128]{2,1,0:T(8,128)(2,1)}), bf16[8,80,128]{2,1,0:T(8,128)(2,1)S(1)}, u32[]{:S(2)}, u32[]{:S(2)}) async-start(bf16[8,80,128]{2,1,0:T(8,128)(2,1)} %message.1), calls=%async_computation | async-start | bytes 327680 | tf_op jit(solution)/shard_map/all_to_all | solution.py:283
  14.9 0.5 %collective-permute-start.5 = (bf16[4,16,128]{2,1,0:T(8,128)(2,1)S(1)}, bf16[4,16,128]{2,1,0:T(8,128)(2,1)S(1)}, u32[]{:S(2)}, u32[]{:S(2)}) collective-permute-start(bf16[4,16,128]{2,1,0:T(8,128)(2,1)S(1)} %spectra.1.spectra_ref.own_ref), channel_id=1, source_target_pairs={{0,24},{8,16},{16,8},{24,0},{1,25},{9,17},{17,9},{25,1},{2,26},{10... | collective-permute-start | bytes 49160 | tf_op jit(solution)/shard_map/ppermute | solution.py:270
  15.5 0.9 %collective-permute-start.4 = (bf16[4,16,128]{2,1,0:T(8,128)(2,1)S(1)}, bf16[4,16,128]{2,1,0:T(8,128)(2,1)S(1)}, u32[]{:S(2)}, u32[]{:S(2)}) collective-permute-start(bf16[4,16,128]{2,1,0:T(8,128)(2,1)S(1)} %spectra.1.spectra_ref.own_ref), channel_id=1, source_target_pairs={{0,16},{8,24},{16,0},{24,8},{1,17},{9,25},{17,1},{25,9},{2,18},{10... | collective-permute-start | bytes 49160 | tf_op jit(solution)/shard_map/ppermute | solution.py:270
  16.3 0.5 %collective-permute-start.3 = (bf16[4,16,128]{2,1,0:T(8,128)(2,1)S(1)}, bf16[4,16,128]{2,1,0:T(8,128)(2,1)S(1)}, u32[]{:S(2)}, u32[]{:S(2)}) collective-permute-start(bf16[4,16,128]{2,1,0:T(8,128)(2,1)S(1)} %spectra.1.spectra_ref.own_ref), channel_id=1, source_target_pairs={{0,8},{8,0},{16,24},{24,16},{1,9},{9,1},{17,25},{25,17},{2,10},{10... | collective-permute-start | bytes 49160 | tf_op jit(solution)/shard_map/ppermute | solution.py:270
  16.8 1.4 %collective-permute-done.5.refs_2_ = bf16[4,16,128]{2,1,0:T(8,128)(2,1)S(1)} collective-permute-done((bf16[4,16,128]{2,1,0:T(8,128)(2,1)S(1)}, bf16[4,16,128]{2,1,0:T(8,128)(2,1)S(1)}, u32[]{:S(2)}, u32[]{:S(2)}) %collective-permute-start.5) | collective-permute-done | bytes 16416 | tf_op jit(solution)/shard_map/ppermute | solution.py:270
  18.2 1.2 %collective-permute-done.4.refs_1_ = bf16[4,16,128]{2,1,0:T(8,128)(2,1)S(1)} collective-permute-done((bf16[4,16,128]{2,1,0:T(8,128)(2,1)S(1)}, bf16[4,16,128]{2,1,0:T(8,128)(2,1)S(1)}, u32[]{:S(2)}, u32[]{:S(2)}) %collective-permute-start.4) | collective-permute-done | bytes 16416 | tf_op jit(solution)/shard_map/ppermute | solution.py:270
  19.4 0.0 collective-permute-done.3.refs_0_
  19.4 0.1 all-to-all-done.gathered_ref
  19.4 0.9 %cross.1 = bf16[2,4,64,128]{3,2,1,0:T(8,128)(2,1)} custom-call(bf16[8,80,128]{2,1,0:T(8,128)(2,1)S(1)} %all-to-all-done.gathered_ref, bf16[4,16,128]{2,1,0:T(8,128)(2,1)S(1)} %spectra.1.spectra_ref.own_ref, bf16[4,16,128]{2,1,0:T(8,128)(2,1)S(1)} %collective-permute-done.3.refs_0_, bf16[4,16,128]{2,1,0:T(8,128)(2,1)S(1)} %collective-permute-done.4.refs_1_, ...), custom_call_target="tpu_custom_call" | custom-call | tf_op jit(solution)/shard_map/cross/pallas_call | solution.py:285
Async XLA Ops:
  1.8 5.7 %collective-permute-start.2 = (f32[8,128]{1,0:T(8,128)S(1)}, f32[8,128]{1,0:T(8,128)S(1)}, u32[]{:S(2)}, u32[]{:S(2)}) collective-permute-start(f32[8,128]{1,0:T(8,128)S(1)} %get-tuple-element.12.own_ref), channel_id=1, source_target_pairs={{0,24},{8,16},{16,8},{24,0},{1,25},{9,17},{17,9},{25,1},{2,26},{10... | collective-permute-start | bytes 12296 | tf_op jit(solution)/shard_map/ppermute | solution.py:270
  4.2 3.6 %collective-permute-start.1 = (f32[8,128]{1,0:T(8,128)S(1)}, f32[8,128]{1,0:T(8,128)S(1)}, u32[]{:S(2)}, u32[]{:S(2)}) collective-permute-start(f32[8,128]{1,0:T(8,128)S(1)} %get-tuple-element.12.own_ref), channel_id=1, source_target_pairs={{0,16},{8,24},{16,0},{24,8},{1,17},{9,25},{17,1},{25,9},{2,18},{10... | collective-permute-start | bytes 12296 | tf_op jit(solution)/shard_map/ppermute | solution.py:270
  4.9 3.0 %collective-permute-start = (f32[8,128]{1,0:T(8,128)S(1)}, f32[8,128]{1,0:T(8,128)S(1)}, u32[]{:S(2)}, u32[]{:S(2)}) collective-permute-start(f32[8,128]{1,0:T(8,128)S(1)} %get-tuple-element.12.own_ref), channel_id=1, source_target_pairs={{0,8},{8,0},{16,24},{24,16},{1,9},{9,1},{17,25},{25,17},{2,10},{10... | collective-permute-start | bytes 12296 | tf_op jit(solution)/shard_map/ppermute | solution.py:270
  8.5 10.9 %all-to-all-start = ((bf16[8,80,128]{2,1,0:T(8,128)(2,1)}), bf16[8,80,128]{2,1,0:T(8,128)(2,1)S(1)}, u32[]{:S(2)}, u32[]{:S(2)}) async-start(bf16[8,80,128]{2,1,0:T(8,128)(2,1)} %message.1), calls=%async_computation | async-start | bytes 327680 | tf_op jit(solution)/shard_map/all_to_all | solution.py:283
  14.9 3.3 %collective-permute-start.5 = (bf16[4,16,128]{2,1,0:T(8,128)(2,1)S(1)}, bf16[4,16,128]{2,1,0:T(8,128)(2,1)S(1)}, u32[]{:S(2)}, u32[]{:S(2)}) collective-permute-start(bf16[4,16,128]{2,1,0:T(8,128)(2,1)S(1)} %spectra.1.spectra_ref.own_ref), channel_id=1, source_target_pairs={{0,24},{8,16},{16,8},{24,0},{1,25},{9,17},{17,9},{25,1},{2,26},{10... | collective-permute-start | bytes 49160 | tf_op jit(solution)/shard_map/ppermute | solution.py:270
  15.5 3.9 %collective-permute-start.4 = (bf16[4,16,128]{2,1,0:T(8,128)(2,1)S(1)}, bf16[4,16,128]{2,1,0:T(8,128)(2,1)S(1)}, u32[]{:S(2)}, u32[]{:S(2)}) collective-permute-start(bf16[4,16,128]{2,1,0:T(8,128)(2,1)S(1)} %spectra.1.spectra_ref.own_ref), channel_id=1, source_target_pairs={{0,16},{8,24},{16,0},{24,8},{1,17},{9,25},{17,1},{25,9},{2,18},{10... | collective-permute-start | bytes 49160 | tf_op jit(solution)/shard_map/ppermute | solution.py:270
  16.3 3.0 %collective-permute-start.3 = (bf16[4,16,128]{2,1,0:T(8,128)(2,1)S(1)}, bf16[4,16,128]{2,1,0:T(8,128)(2,1)S(1)}, u32[]{:S(2)}, u32[]{:S(2)}) collective-permute-start(bf16[4,16,128]{2,1,0:T(8,128)(2,1)S(1)} %spectra.1.spectra_ref.own_ref), channel_id=1, source_target_pairs={{0,8},{8,0},{16,24},{24,16},{1,9},{9,1},{17,25},{25,17},{2,10},{10... | collective-permute-start | bytes 49160 | tf_op jit(solution)/shard_map/ppermute | solution.py:270

commit v4 on v3

--- a/solution.py
+++ b/solution.py
@@ -90,7 +90,7 @@
                 value = x_ref[channel, :, tile * 128 : (tile + 1) * 128].astype(F32)
                 total = total + value * value
     row = jnp.sum(jnp.transpose(total), axis=0, keepdims=True)
-    power_ref[...] = jnp.broadcast_to(jnp.concatenate([row, row], axis=1), power_ref.shape)
+    power_ref[...] = jnp.concatenate([row, row], axis=1)
 
 
 def front(strain_rate, parts=8):
@@ -100,7 +100,7 @@
         out_specs=in_vmem(4),
         out_shape=[
             jax.ShapeDtypeStruct(strain_rate.shape, BF16),
-            jax.ShapeDtypeStruct((8, LANES), F32),
+            jax.ShapeDtypeStruct((1, LANES), F32),
             jax.ShapeDtypeStruct((TILE + 2 * REACH, TILE), BF16),
             jax.ShapeDtypeStruct((4 * PAD, NS), BF16),
         ],
@@ -191,6 +191,7 @@
     power = own_ref[...]
     for ref in power_refs:
         power = power + ref[...]
+    power = jnp.broadcast_to(power, (8, LANES))
     high = power.astype(BF16)
     rest = power - high.astype(F32)
     middle = rest.astype(BF16)
@@ -253,7 +254,7 @@
 
 
 def column_order(col_count):
-    best = [4, 2, 6, 5, 1, 0, 7, 3]
+    best = [4, 2, 3, 6, 5, 1, 0, 7]
     if col_count == len(best):
         return best
     middle = col_count // 2

time: 20.6 us -> 20.6 us (level)
  no operation moved by 1% of the time
where the time goes in v4:
time: 20.6 us; the launch traced here: 20.4 us
  starting transfers between devices  11.4 us (55%)
  Pallas kernels  5.93 us (29%)
  waiting for transfers between devices  3.03 us (15%)
    all_to_all x1, starting transfers between devices, shards(): gathered = lax.all_to_all(message, 'col', 0, 0, axis_index_groups=[order])  6.4 us
    ppermute x6, starting transfers between devices, from_row(): lax.ppermute(value, 'row', [(i, i ^ shift) for i in range(row_count)])  4.98 us
    ppermute x6, waiting for transfers between devices, from_row(): lax.ppermute(value, 'row', [(i, i ^ shift) for i in range(row_count)])  2.97 us
    pallas_call x1, Pallas kernels, local_spectra(): pl.pallas_call(functools.partial(spectra_kernel, block), in_specs=in_vmem...  2.53 us
    pallas_call x1, Pallas kernels, front(): pl.pallas_call(front_kernel, in_specs=[pl.BlockSpec(memory_space=pltpu.HB...  1.79 us
    pallas_call x1, Pallas kernels, shards(): pl.pallas_call(functools.partial(cross_kernel, order, row_count * col_cou...  0.92 us
    pallas_call x1, Pallas kernels, shards(): pl.pallas_call(message_kernel, in_specs=in_vmem(1 + row_count), out_specs...  0.68 us
  transfers between devices with their start and end apart: 7, of which 4 were waited for; matrix products, arithmetic and copies ran while one was open for 0% of the time, Pallas kernels for 12%

profile of v4, /device:TPU:0, one launch (start us, length us, event | category | flops | bytes accessed | tf_op | source)
XLA Modules:
  0.0 20.4 jit_solution(16882336886517019419)
XLA Ops:
  0.0 1.8 %front.1 = (bf16[16,64,1024]{2,1,0:T(8,128)(2,1)S(1)}, f32[1,128]{1,0:T(1,128)S(1)}, bf16[512,256]{1,0:T(8,128)(2,1)S(1)}, bf16[64,1024]{1,0:T(8,128)(2,1)S(1)}) custom-call(bf16[16,64,1024]{2,1,0:T(8,128)(2,1)} %x_hbm.1), custom_call_target="tpu_custom_call" | custom-call | tf_op jit(solution)/shard_map/front/pallas_call | solution.py:97
  1.8 2.4 %collective-permute-start.2 = (f32[1,128]{1,0:T(1,128)S(1)}, f32[1,128]{1,0:T(1,128)S(1)}, u32[]{:S(2)}, u32[]{:S(2)}) collective-permute-start(f32[1,128]{1,0:T(1,128)S(1)} %get-tuple-element.12.own_ref), channel_id=1, source_target_pairs={{0,24},{8,16},{16,8},{24,0},{1,25},{9,17},{17,9},{25,1},{2,26},{10... | collective-permute-start | bytes 1544 | tf_op jit(solution)/shard_map/ppermute | solution.py:271
  4.2 0.6 %collective-permute-start.1 = (f32[1,128]{1,0:T(1,128)S(1)}, f32[1,128]{1,0:T(1,128)S(1)}, u32[]{:S(2)}, u32[]{:S(2)}) collective-permute-start(f32[1,128]{1,0:T(1,128)S(1)} %get-tuple-element.12.own_ref), channel_id=1, source_target_pairs={{0,16},{8,24},{16,0},{24,8},{1,17},{9,25},{17,1},{25,9},{2,18},{10... | collective-permute-start | bytes 1544 | tf_op jit(solution)/shard_map/ppermute | solution.py:271
  4.9 0.0 collective-permute-start
  4.9 2.5 %spectra.1.spectra_ref.own_ref = bf16[4,16,128]{2,1,0:T(8,128)(2,1)S(1)} custom-call(bf16[16,64,1024]{2,1,0:T(8,128)(2,1)S(1)} %get-tuple-element.9.x_ref, bf16[512,256]{1,0:T(8,128)(2,1)S(1)} %get-tuple-element.10.band, bf16[64,1024]{1,0:T(8,128)(2,1)S(1)} %get-tuple-element.11.dft), custom_call_target="tpu_custom_call" | custom-call | tf_op jit(solution)/shard_map/spectra/pallas_call | solution.py:177
  7.5 0.0 collective-permute-done.2.refs_2_
  7.5 0.3 %collective-permute-done.1.refs_1_ = f32[1,128]{1,0:T(1,128)S(1)} collective-permute-done((f32[1,128]{1,0:T(1,128)S(1)}, f32[1,128]{1,0:T(1,128)S(1)}, u32[]{:S(2)}, u32[]{:S(2)}) %collective-permute-start.1) | collective-permute-done | bytes 544 | tf_op jit(solution)/shard_map/ppermute | solution.py:271
  7.8 0.0 collective-permute-done.refs_0_
  7.8 0.7 %message.1 = bf16[8,80,128]{2,1,0:T(8,128)(2,1)} custom-call(bf16[4,16,128]{2,1,0:T(8,128)(2,1)S(1)} %spectra.1.spectra_ref.own_ref, f32[1,128]{1,0:T(1,128)S(1)} %get-tuple-element.12.own_ref, f32[1,128]{1,0:T(1,128)S(1)} %collective-permute-done.refs_0_, f32[1,128]{1,0:T(1,128)S(1)} %collective-permute-done.1.refs_1_, ...), custom_call_target="tpu_custom_call" | custom-call | tf_op jit(solution)/shard_map/message/pallas_call | solution.py:276
  8.5 6.4 %all-to-all-start = ((bf16[8,80,128]{2,1,0:T(8,128)(2,1)}), bf16[8,80,128]{2,1,0:T(8,128)(2,1)S(1)}, u32[]{:S(2)}, u32[]{:S(2)}) async-start(bf16[8,80,128]{2,1,0:T(8,128)(2,1)} %message.1), calls=%async_computation | async-start | bytes 327680 | tf_op jit(solution)/shard_map/all_to_all | solution.py:284
  14.9 0.6 %collective-permute-start.5 = (bf16[4,16,128]{2,1,0:T(8,128)(2,1)S(1)}, bf16[4,16,128]{2,1,0:T(8,128)(2,1)S(1)}, u32[]{:S(2)}, u32[]{:S(2)}) collective-permute-start(bf16[4,16,128]{2,1,0:T(8,128)(2,1)S(1)} %spectra.1.spectra_ref.own_ref), channel_id=1, source_target_pairs={{0,24},{8,16},{16,8},{24,0},{1,25},{9,17},{17,9},{25,1},{2,26},{10... | collective-permute-start | bytes 49160 | tf_op jit(solution)/shard_map/ppermute | solution.py:271
  15.5 0.9 %collective-permute-start.4 = (bf16[4,16,128]{2,1,0:T(8,128)(2,1)S(1)}, bf16[4,16,128]{2,1,0:T(8,128)(2,1)S(1)}, u32[]{:S(2)}, u32[]{:S(2)}) collective-permute-start(bf16[4,16,128]{2,1,0:T(8,128)(2,1)S(1)} %spectra.1.spectra_ref.own_ref), channel_id=1, source_target_pairs={{0,16},{8,24},{16,0},{24,8},{1,17},{9,25},{17,1},{25,9},{2,18},{10... | collective-permute-start | bytes 49160 | tf_op jit(solution)/shard_map/ppermute | solution.py:271
  16.3 0.4 %collective-permute-start.3 = (bf16[4,16,128]{2,1,0:T(8,128)(2,1)S(1)}, bf16[4,16,128]{2,1,0:T(8,128)(2,1)S(1)}, u32[]{:S(2)}, u32[]{:S(2)}) collective-permute-start(bf16[4,16,128]{2,1,0:T(8,128)(2,1)S(1)} %spectra.1.spectra_ref.own_ref), channel_id=1, source_target_pairs={{0,8},{8,0},{16,24},{24,16},{1,9},{9,1},{17,25},{25,17},{2,10},{10... | collective-permute-start | bytes 49160 | tf_op jit(solution)/shard_map/ppermute | solution.py:271
  16.7 1.5 %collective-permute-done.5.refs_2_ = bf16[4,16,128]{2,1,0:T(8,128)(2,1)S(1)} collective-permute-done((bf16[4,16,128]{2,1,0:T(8,128)(2,1)S(1)}, bf16[4,16,128]{2,1,0:T(8,128)(2,1)S(1)}, u32[]{:S(2)}, u32[]{:S(2)}) %collective-permute-start.5) | collective-permute-done | bytes 16416 | tf_op jit(solution)/shard_map/ppermute | solution.py:271
  18.2 1.2 %collective-permute-done.4.refs_1_ = bf16[4,16,128]{2,1,0:T(8,128)(2,1)S(1)} collective-permute-done((bf16[4,16,128]{2,1,0:T(8,128)(2,1)S(1)}, bf16[4,16,128]{2,1,0:T(8,128)(2,1)S(1)}, u32[]{:S(2)}, u32[]{:S(2)}) %collective-permute-start.4) | collective-permute-done | bytes 16416 | tf_op jit(solution)/shard_map/ppermute | solution.py:271
  19.4 0.0 collective-permute-done.3.refs_0_
  19.4 0.1 all-to-all-done.gathered_ref
  19.4 0.9 %cross.1 = bf16[2,4,64,128]{3,2,1,0:T(8,128)(2,1)} custom-call(bf16[8,80,128]{2,1,0:T(8,128)(2,1)S(1)} %all-to-all-done.gathered_ref, bf16[4,16,128]{2,1,0:T(8,128)(2,1)S(1)} %spectra.1.spectra_ref.own_ref, bf16[4,16,128]{2,1,0:T(8,128)(2,1)S(1)} %collective-permute-done.3.refs_0_, bf16[4,16,128]{2,1,0:T(8,128)(2,1)S(1)} %collective-permute-done.4.refs_1_, ...), custom_call_target="tpu_custom_call" | custom-call | tf_op jit(solution)/shard_map/cross/pallas_call | solution.py:286
Async XLA Ops:
  1.8 5.7 %collective-permute-start.2 = (f32[1,128]{1,0:T(1,128)S(1)}, f32[1,128]{1,0:T(1,128)S(1)}, u32[]{:S(2)}, u32[]{:S(2)}) collective-permute-start(f32[1,128]{1,0:T(1,128)S(1)} %get-tuple-element.12.own_ref), channel_id=1, source_target_pairs={{0,24},{8,16},{16,8},{24,0},{1,25},{9,17},{17,9},{25,1},{2,26},{10... | collective-permute-start | bytes 1544 | tf_op jit(solution)/shard_map/ppermute | solution.py:271
  4.2 3.5 %collective-permute-start.1 = (f32[1,128]{1,0:T(1,128)S(1)}, f32[1,128]{1,0:T(1,128)S(1)}, u32[]{:S(2)}, u32[]{:S(2)}) collective-permute-start(f32[1,128]{1,0:T(1,128)S(1)} %get-tuple-element.12.own_ref), channel_id=1, source_target_pairs={{0,16},{8,24},{16,0},{24,8},{1,17},{9,25},{17,1},{25,9},{2,18},{10... | collective-permute-start | bytes 1544 | tf_op jit(solution)/shard_map/ppermute | solution.py:271
  4.9 2.9 %collective-permute-start = (f32[1,128]{1,0:T(1,128)S(1)}, f32[1,128]{1,0:T(1,128)S(1)}, u32[]{:S(2)}, u32[]{:S(2)}) collective-permute-start(f32[1,128]{1,0:T(1,128)S(1)} %get-tuple-element.12.own_ref), channel_id=1, source_target_pairs={{0,8},{8,0},{16,24},{24,16},{1,9},{9,1},{17,25},{25,17},{2,10},{10... | collective-permute-start | bytes 1544 | tf_op jit(solution)/shard_map/ppermute | solution.py:271
  8.5 11.0 %all-to-all-start = ((bf16[8,80,128]{2,1,0:T(8,128)(2,1)}), bf16[8,80,128]{2,1,0:T(8,128)(2,1)S(1)}, u32[]{:S(2)}, u32[]{:S(2)}) async-start(bf16[8,80,128]{2,1,0:T(8,128)(2,1)} %message.1), calls=%async_computation | async-start | bytes 327680 | tf_op jit(solution)/shard_map/all_to_all | solution.py:284
  14.9 3.3 %collective-permute-start.5 = (bf16[4,16,128]{2,1,0:T(8,128)(2,1)S(1)}, bf16[4,16,128]{2,1,0:T(8,128)(2,1)S(1)}, u32[]{:S(2)}, u32[]{:S(2)}) collective-permute-start(bf16[4,16,128]{2,1,0:T(8,128)(2,1)S(1)} %spectra.1.spectra_ref.own_ref), channel_id=1, source_target_pairs={{0,24},{8,16},{16,8},{24,0},{1,25},{9,17},{17,9},{25,1},{2,26},{10... | collective-permute-start | bytes 49160 | tf_op jit(solution)/shard_map/ppermute | solution.py:271
  15.5 3.9 %collective-permute-start.4 = (bf16[4,16,128]{2,1,0:T(8,128)(2,1)S(1)}, bf16[4,16,128]{2,1,0:T(8,128)(2,1)S(1)}, u32[]{:S(2)}, u32[]{:S(2)}) collective-permute-start(bf16[4,16,128]{2,1,0:T(8,128)(2,1)S(1)} %spectra.1.spectra_ref.own_ref), channel_id=1, source_target_pairs={{0,16},{8,24},{16,0},{24,8},{1,17},{9,25},{17,1},{25,9},{2,18},{10... | collective-permute-start | bytes 49160 | tf_op jit(solution)/shard_map/ppermute | solution.py:271
  16.3 3.0 %collective-permute-start.3 = (bf16[4,16,128]{2,1,0:T(8,128)(2,1)S(1)}, bf16[4,16,128]{2,1,0:T(8,128)(2,1)S(1)}, u32[]{:S(2)}, u32[]{:S(2)}) collective-permute-start(bf16[4,16,128]{2,1,0:T(8,128)(2,1)S(1)} %spectra.1.spectra_ref.own_ref), channel_id=1, source_target_pairs={{0,8},{8,0},{16,24},{24,16},{1,9},{9,1},{17,25},{25,17},{2,10},{10... | collective-permute-start | bytes 49160 | tf_op jit(solution)/shard_map/ppermute | solution.py:271

commit v5 on v4

--- a/solution.py
+++ b/solution.py
@@ -217,8 +217,7 @@
         value = parts[0:1] + (parts[1:2] + parts[2:3])
         power = value if power is None else power + value
     power = power / (channels * members * samples)
-    gain = 1.0 / jnp.sqrt(power + 1e-05)
-    gain_square = gain * gain
+    gain_square = 1.0 / (power + 1e-05)
     lane = lax.broadcasted_iota(jnp.int32, (1, LANES), 1)
     turned_gain = jnp.where(lane < W, -gain_square, gain_square)
     me = lax.axis_index("row")

time: 20.6 us -> 20.6 us (level)
  no operation moved by 1% of the time
where the time goes in v5:
time: 20.6 us; the launch traced here: 20.4 us
  starting transfers between devices  11.4 us (55%)
  Pallas kernels  5.93 us (29%)
  waiting for transfers between devices  3.03 us (15%)
    all_to_all x1, starting transfers between devices, shards(): gathered = lax.all_to_all(message, 'col', 0, 0, axis_index_groups=[order])  6.4 us
    ppermute x6, starting transfers between devices, from_row(): lax.ppermute(value, 'row', [(i, i ^ shift) for i in range(row_count)])  4.98 us
    ppermute x6, waiting for transfers between devices, from_row(): lax.ppermute(value, 'row', [(i, i ^ shift) for i in range(row_count)])  2.97 us
    pallas_call x1, Pallas kernels, local_spectra(): pl.pallas_call(functools.partial(spectra_kernel, block), in_specs=in_vmem...  2.53 us
    pallas_call x1, Pallas kernels, front(): pl.pallas_call(front_kernel, in_specs=[pl.BlockSpec(memory_space=pltpu.HB...  1.79 us
    pallas_call x1, Pallas kernels, shards(): pl.pallas_call(functools.partial(cross_kernel, order, row_count * col_cou...  0.92 us
    pallas_call x1, Pallas kernels, shards(): pl.pallas_call(message_kernel, in_specs=in_vmem(1 + row_count), out_specs...  0.68 us
  transfers between devices with their start and end apart: 7, of which 4 were waited for; matrix products, arithmetic and copies ran while one was open for 0% of the time, Pallas kernels for 12%

profile of v5, /device:TPU:0, one launch (start us, length us, event | category | flops | bytes accessed | tf_op | source)
XLA Modules:
  0.0 20.4 jit_solution(15866664198290108712)
XLA Ops:
  0.0 1.8 %front.1 = (bf16[16,64,1024]{2,1,0:T(8,128)(2,1)S(1)}, f32[1,128]{1,0:T(1,128)S(1)}, bf16[512,256]{1,0:T(8,128)(2,1)S(1)}, bf16[64,1024]{1,0:T(8,128)(2,1)S(1)}) custom-call(bf16[16,64,1024]{2,1,0:T(8,128)(2,1)} %x_hbm.1), custom_call_target="tpu_custom_call" | custom-call | tf_op jit(solution)/shard_map/front/pallas_call | solution.py:97
  1.8 2.4 %collective-permute-start.2 = (f32[1,128]{1,0:T(1,128)S(1)}, f32[1,128]{1,0:T(1,128)S(1)}, u32[]{:S(2)}, u32[]{:S(2)}) collective-permute-start(f32[1,128]{1,0:T(1,128)S(1)} %get-tuple-element.12.own_ref), channel_id=1, source_target_pairs={{0,24},{8,16},{16,8},{24,0},{1,25},{9,17},{17,9},{25,1},{2,26},{10... | collective-permute-start | bytes 1544 | tf_op jit(solution)/shard_map/ppermute | solution.py:270
  4.2 0.6 %collective-permute-start.1 = (f32[1,128]{1,0:T(1,128)S(1)}, f32[1,128]{1,0:T(1,128)S(1)}, u32[]{:S(2)}, u32[]{:S(2)}) collective-permute-start(f32[1,128]{1,0:T(1,128)S(1)} %get-tuple-element.12.own_ref), channel_id=1, source_target_pairs={{0,16},{8,24},{16,0},{24,8},{1,17},{9,25},{17,1},{25,9},{2,18},{10... | collective-permute-start | bytes 1544 | tf_op jit(solution)/shard_map/ppermute | solution.py:270
  4.9 0.0 collective-permute-start
  4.9 2.5 %spectra.1.spectra_ref.own_ref = bf16[4,16,128]{2,1,0:T(8,128)(2,1)S(1)} custom-call(bf16[16,64,1024]{2,1,0:T(8,128)(2,1)S(1)} %get-tuple-element.9.x_ref, bf16[512,256]{1,0:T(8,128)(2,1)S(1)} %get-tuple-element.10.band, bf16[64,1024]{1,0:T(8,128)(2,1)S(1)} %get-tuple-element.11.dft), custom_call_target="tpu_custom_call" | custom-call | tf_op jit(solution)/shard_map/spectra/pallas_call | solution.py:177
  7.5 0.0 collective-permute-done.2.refs_2_
  7.5 0.3 %collective-permute-done.1.refs_1_ = f32[1,128]{1,0:T(1,128)S(1)} collective-permute-done((f32[1,128]{1,0:T(1,128)S(1)}, f32[1,128]{1,0:T(1,128)S(1)}, u32[]{:S(2)}, u32[]{:S(2)}) %collective-permute-start.1) | collective-permute-done | bytes 544 | tf_op jit(solution)/shard_map/ppermute | solution.py:270
  7.8 0.0 collective-permute-done.refs_0_
  7.8 0.7 %message.1 = bf16[8,80,128]{2,1,0:T(8,128)(2,1)} custom-call(bf16[4,16,128]{2,1,0:T(8,128)(2,1)S(1)} %spectra.1.spectra_ref.own_ref, f32[1,128]{1,0:T(1,128)S(1)} %get-tuple-element.12.own_ref, f32[1,128]{1,0:T(1,128)S(1)} %collective-permute-done.refs_0_, f32[1,128]{1,0:T(1,128)S(1)} %collective-permute-done.1.refs_1_, ...), custom_call_target="tpu_custom_call" | custom-call | tf_op jit(solution)/shard_map/message/pallas_call | solution.py:275
  8.5 6.4 %all-to-all-start = ((bf16[8,80,128]{2,1,0:T(8,128)(2,1)}), bf16[8,80,128]{2,1,0:T(8,128)(2,1)S(1)}, u32[]{:S(2)}, u32[]{:S(2)}) async-start(bf16[8,80,128]{2,1,0:T(8,128)(2,1)} %message.1), calls=%async_computation | async-start | bytes 327680 | tf_op jit(solution)/shard_map/all_to_all | solution.py:283
  14.9 0.6 %collective-permute-start.5 = (bf16[4,16,128]{2,1,0:T(8,128)(2,1)S(1)}, bf16[4,16,128]{2,1,0:T(8,128)(2,1)S(1)}, u32[]{:S(2)}, u32[]{:S(2)}) collective-permute-start(bf16[4,16,128]{2,1,0:T(8,128)(2,1)S(1)} %spectra.1.spectra_ref.own_ref), channel_id=1, source_target_pairs={{0,24},{8,16},{16,8},{24,0},{1,25},{9,17},{17,9},{25,1},{2,26},{10... | collective-permute-start | bytes 49160 | tf_op jit(solution)/shard_map/ppermute | solution.py:270
  15.5 0.9 %collective-permute-start.4 = (bf16[4,16,128]{2,1,0:T(8,128)(2,1)S(1)}, bf16[4,16,128]{2,1,0:T(8,128)(2,1)S(1)}, u32[]{:S(2)}, u32[]{:S(2)}) collective-permute-start(bf16[4,16,128]{2,1,0:T(8,128)(2,1)S(1)} %spectra.1.spectra_ref.own_ref), channel_id=1, source_target_pairs={{0,16},{8,24},{16,0},{24,8},{1,17},{9,25},{17,1},{25,9},{2,18},{10... | collective-permute-start | bytes 49160 | tf_op jit(solution)/shard_map/ppermute | solution.py:270
  16.3 0.4 %collective-permute-start.3 = (bf16[4,16,128]{2,1,0:T(8,128)(2,1)S(1)}, bf16[4,16,128]{2,1,0:T(8,128)(2,1)S(1)}, u32[]{:S(2)}, u32[]{:S(2)}) collective-permute-start(bf16[4,16,128]{2,1,0:T(8,128)(2,1)S(1)} %spectra.1.spectra_ref.own_ref), channel_id=1, source_target_pairs={{0,8},{8,0},{16,24},{24,16},{1,9},{9,1},{17,25},{25,17},{2,10},{10... | collective-permute-start | bytes 49160 | tf_op jit(solution)/shard_map/ppermute | solution.py:270
  16.7 1.5 %collective-permute-done.5.refs_2_ = bf16[4,16,128]{2,1,0:T(8,128)(2,1)S(1)} collective-permute-done((bf16[4,16,128]{2,1,0:T(8,128)(2,1)S(1)}, bf16[4,16,128]{2,1,0:T(8,128)(2,1)S(1)}, u32[]{:S(2)}, u32[]{:S(2)}) %collective-permute-start.5) | collective-permute-done | bytes 16416 | tf_op jit(solution)/shard_map/ppermute | solution.py:270
  18.2 1.2 %collective-permute-done.4.refs_1_ = bf16[4,16,128]{2,1,0:T(8,128)(2,1)S(1)} collective-permute-done((bf16[4,16,128]{2,1,0:T(8,128)(2,1)S(1)}, bf16[4,16,128]{2,1,0:T(8,128)(2,1)S(1)}, u32[]{:S(2)}, u32[]{:S(2)}) %collective-permute-start.4) | collective-permute-done | bytes 16416 | tf_op jit(solution)/shard_map/ppermute | solution.py:270
  19.4 0.0 collective-permute-done.3.refs_0_
  19.4 0.1 all-to-all-done.gathered_ref
  19.4 0.9 %cross.1 = bf16[2,4,64,128]{3,2,1,0:T(8,128)(2,1)} custom-call(bf16[8,80,128]{2,1,0:T(8,128)(2,1)S(1)} %all-to-all-done.gathered_ref, bf16[4,16,128]{2,1,0:T(8,128)(2,1)S(1)} %spectra.1.spectra_ref.own_ref, bf16[4,16,128]{2,1,0:T(8,128)(2,1)S(1)} %collective-permute-done.3.refs_0_, bf16[4,16,128]{2,1,0:T(8,128)(2,1)S(1)} %collective-permute-done.4.refs_1_, ...), custom_call_target="tpu_custom_call" | custom-call | tf_op jit(solution)/shard_map/cross/pallas_call | solution.py:285
Async XLA Ops:
  1.8 5.7 %collective-permute-start.2 = (f32[1,128]{1,0:T(1,128)S(1)}, f32[1,128]{1,0:T(1,128)S(1)}, u32[]{:S(2)}, u32[]{:S(2)}) collective-permute-start(f32[1,128]{1,0:T(1,128)S(1)} %get-tuple-element.12.own_ref), channel_id=1, source_target_pairs={{0,24},{8,16},{16,8},{24,0},{1,25},{9,17},{17,9},{25,1},{2,26},{10... | collective-permute-start | bytes 1544 | tf_op jit(solution)/shard_map/ppermute | solution.py:270
  4.2 3.5 %collective-permute-start.1 = (f32[1,128]{1,0:T(1,128)S(1)}, f32[1,128]{1,0:T(1,128)S(1)}, u32[]{:S(2)}, u32[]{:S(2)}) collective-permute-start(f32[1,128]{1,0:T(1,128)S(1)} %get-tuple-element.12.own_ref), channel_id=1, source_target_pairs={{0,16},{8,24},{16,0},{24,8},{1,17},{9,25},{17,1},{25,9},{2,18},{10... | collective-permute-start | bytes 1544 | tf_op jit(solution)/shard_map/ppermute | solution.py:270
  4.9 2.9 %collective-permute-start = (f32[1,128]{1,0:T(1,128)S(1)}, f32[1,128]{1,0:T(1,128)S(1)}, u32[]{:S(2)}, u32[]{:S(2)}) collective-permute-start(f32[1,128]{1,0:T(1,128)S(1)} %get-tuple-element.12.own_ref), channel_id=1, source_target_pairs={{0,8},{8,0},{16,24},{24,16},{1,9},{9,1},{17,25},{25,17},{2,10},{10... | collective-permute-start | bytes 1544 | tf_op jit(solution)/shard_map/ppermute | solution.py:270
  8.5 11.0 %all-to-all-start = ((bf16[8,80,128]{2,1,0:T(8,128)(2,1)}), bf16[8,80,128]{2,1,0:T(8,128)(2,1)S(1)}, u32[]{:S(2)}, u32[]{:S(2)}) async-start(bf16[8,80,128]{2,1,0:T(8,128)(2,1)} %message.1), calls=%async_computation | async-start | bytes 327680 | tf_op jit(solution)/shard_map/all_to_all | solution.py:283
  14.9 3.3 %collective-permute-start.5 = (bf16[4,16,128]{2,1,0:T(8,128)(2,1)S(1)}, bf16[4,16,128]{2,1,0:T(8,128)(2,1)S(1)}, u32[]{:S(2)}, u32[]{:S(2)}) collective-permute-start(bf16[4,16,128]{2,1,0:T(8,128)(2,1)S(1)} %spectra.1.spectra_ref.own_ref), channel_id=1, source_target_pairs={{0,24},{8,16},{16,8},{24,0},{1,25},{9,17},{17,9},{25,1},{2,26},{10... | collective-permute-start | bytes 49160 | tf_op jit(solution)/shard_map/ppermute | solution.py:270
  15.5 3.9 %collective-permute-start.4 = (bf16[4,16,128]{2,1,0:T(8,128)(2,1)S(1)}, bf16[4,16,128]{2,1,0:T(8,128)(2,1)S(1)}, u32[]{:S(2)}, u32[]{:S(2)}) collective-permute-start(bf16[4,16,128]{2,1,0:T(8,128)(2,1)S(1)} %spectra.1.spectra_ref.own_ref), channel_id=1, source_target_pairs={{0,16},{8,24},{16,0},{24,8},{1,17},{9,25},{17,1},{25,9},{2,18},{10... | collective-permute-start | bytes 49160 | tf_op jit(solution)/shard_map/ppermute | solution.py:270
  16.3 3.0 %collective-permute-start.3 = (bf16[4,16,128]{2,1,0:T(8,128)(2,1)S(1)}, bf16[4,16,128]{2,1,0:T(8,128)(2,1)S(1)}, u32[]{:S(2)}, u32[]{:S(2)}) collective-permute-start(bf16[4,16,128]{2,1,0:T(8,128)(2,1)S(1)} %spectra.1.spectra_ref.own_ref), channel_id=1, source_target_pairs={{0,8},{8,0},{16,24},{24,16},{1,9},{9,1},{17,25},{25,17},{2,10},{10... | collective-permute-start | bytes 49160 | tf_op jit(solution)/shard_map/ppermute | solution.py:270
